TPU v7x, 32 devices: a whole 2x2x4 slice. The times are simulated.
32 devices in a mesh: ctx: 2 (over x), exp: 16 (over z, y, core).
Axes of the slice: x: 2, y: 2, z: 4, core: 2. Of those that a mesh axis runs over, the one named last changes fastest.
Arguments:
- tokens: bfloat16 [256, 4096], P('ctx', 'exp'), may hold values from -6 to 6
- input_weight: bfloat16 [4096, 8192], P('ctx', 'exp'), may hold values from -0.09375 to 0.09375
- gate_weight: bfloat16 [4096, 8192], P('ctx', 'exp'), may hold values from -0.09375 to 0.09375
- conv_weight: float32 [4, 8192], P(None, 'exp'), may hold values from -3 to 3
- conv_bias: float32 [8192], P('exp'), may hold values from -3 to 3
- state_weight: bfloat16 [8192, 32], P('exp'), may hold values from -0.0078125 to 0.0078125
- step_size: float32 [256, 8192], P('ctx', 'exp'), may hold values from 0 to 1, as said below
- skip_gain: float32 [8192], P('exp'), may hold values from 0.5 to 2
- output_weight: bfloat16 [8192, 4096], P('exp', 'ctx'), may hold values from -0.0625 to 0.0625
- norm_gain: float32 [4096], replicated, may hold values from 0.1 to 1.9
- router_weight: bfloat16 [4096, 16], replicated, may hold values from -0.09375 to 0.09375
- expert_gate: bfloat16 [16, 7168, 4096], P('exp', 'ctx'), may hold values from -0.09375 to 0.09375
- expert_up: bfloat16 [16, 7168, 4096], P('exp', 'ctx'), may hold values from -0.09375 to 0.09375
- expert_down: bfloat16 [16, 7168, 4096], P('exp', 'ctx'), may hold values from -0.0625 to 0.0625
- expert_ids: int32 [256, 2], P(('ctx', 'exp')), may hold values from 0 to 15, all different within a row; in each aligned block of 8 rows (0 to 7, 8 to 15, ...) at most 2 rows name the same one
Outputs:
- layer_out: bfloat16 [256, 4096], P(('ctx', 'exp'))
Inputs may be any that keep to these rules, and one draw needn't show every extreme that they name: `expert_ids`: each token names 2 different experts; in each aligned block of 8 tokens no expert is named by more than 2 tokens. `step_size`: a positive rate for each token and channel.
All inputs are finite; a program needn't handle non-finite values.
Results may differ from a plain program's by a relative error of at most 0.028.
Values may be sent and summed in bfloat16 or wider, within the bound.
No kernel may reach another device: no remote copies, remote signals or barrier semaphores. Data moves between devices by JAX's collectives and lax.ppermute only.
A program may use at most 192 MiB of HBM per device.

v0:
```python
import jax
import jax.numpy as jnp
from jax import lax
from jax.sharding import PartitionSpec as P

STATE = 16
CONV = 4
TOP = 2
CAP = 2


precise = lax.Precision.HIGHEST


def shifted(shard, axis, by):
    devices = lax.axis_size(axis)
    pairs = [(i, i + by) for i in range(devices) if 0 <= i + by < devices]
    return lax.ppermute(shard, axis, pairs)


def causal_part(scores, decay_block, input_block):
    length = decay_block.shape[0]
    causal = (jnp.arange(length)[:, None] >= jnp.arange(length)[None, :])[:, :, None]
    distance = decay_block[:, None, :] - decay_block[None, :, :]
    weight = jnp.where(causal, jnp.exp(-jnp.where(causal, distance, 0.0)), 0.0)
    return jnp.einsum("ts,tsc,sc->tc", scores, weight, input_block, precision=precise)


def local(
    tokens,
    input_weight,
    gate_weight,
    conv_weight,
    conv_bias,
    state_weight,
    step_size,
    skip_gain,
    output_weight,
    norm_gain,
    router_weight,
    expert_gate,
    expert_up,
    expert_down,
    expert_ids,
):
    whole_stretch = lax.all_gather(tokens, "exp", axis=1, tiled=True)
    stretch_rows = whole_stretch.shape[0]
    inner_width = input_weight.shape[1]
    inner_x = jnp.dot(
        whole_stretch,
        lax.all_gather(input_weight, "ctx", axis=0, tiled=True),
        preferred_element_type=jnp.float32,
    )
    inner_z = jnp.dot(
        whole_stretch,
        lax.all_gather(gate_weight, "ctx", axis=0, tiled=True),
        preferred_element_type=jnp.float32,
    )
    inner_x = inner_x.astype(jnp.bfloat16)
    inner_z = inner_z.astype(jnp.bfloat16)
    earlier_rows = shifted(inner_x[stretch_rows - (CONV - 1) :], "ctx", 1)
    extended = jnp.concatenate([earlier_rows, inner_x], 0).astype(jnp.float32)
    filtered = jnp.broadcast_to(conv_bias[None, :], (stretch_rows, inner_width))
    for offset in range(CONV):
        filtered = (
            filtered + conv_weight[offset][None, :] * extended[offset : offset + stretch_rows]
        )
    mixer_in = jax.nn.silu(filtered).astype(jnp.bfloat16)
    mixer_wide = mixer_in.astype(jnp.float32)
    projections = lax.psum(
        jnp.dot(mixer_in, state_weight, preferred_element_type=jnp.float32), "exp"
    )
    input_gain = projections[:, :STATE]
    readout = projections[:, STATE:]
    cumulative = jnp.cumsum(step_size, 0)
    scores = jnp.dot(readout, input_gain.T, precision=precise)
    block_width = 128
    block_count = inner_width // block_width
    decay_blocks = cumulative.reshape(stretch_rows, block_count, block_width).transpose(1, 0, 2)
    incoming_slabs = mixer_wide.reshape(stretch_rows, block_count, block_width).transpose(1, 0, 2)
    inside = lax.map(
        lambda paired: causal_part(scores, paired[0], paired[1]), (decay_blocks, incoming_slabs)
    )
    inside = inside.transpose(1, 0, 2).reshape(stretch_rows, inner_width)
    total_decay = cumulative[stretch_rows - 1]
    tail_weight = jnp.exp(-(total_decay[None, :] - cumulative)) * mixer_wide
    local_end = jnp.dot(tail_weight.T, input_gain, precision=precise)
    stretch_keep = jnp.exp(-total_decay)

    def relay_step(turn_index, received):
        leaving = stretch_keep[:, None] * received + local_end
        return shifted(leaving, "ctx", 1)

    entering = lax.fori_loop(0, lax.axis_size("ctx") - 1, relay_step, jnp.zeros_like(local_end))
    carried = jnp.exp(-cumulative) * jnp.dot(readout, entering.T, precision=precise)
    mixed_state = (inside + carried + skip_gain[None, :] * mixer_wide) * jax.nn.silu(
        inner_z.astype(jnp.float32)
    )
    blender_result = mixed_state.astype(jnp.bfloat16)
    row_count = expert_ids.shape[0]
    start_row = lax.axis_index("exp") * row_count
    own_tokens = lax.dynamic_slice_in_dim(whole_stretch, start_row, row_count, 0)
    out_whole = lax.all_gather(output_weight, "ctx", axis=1, tiled=True)
    projected = lax.psum_scatter(
        jnp.dot(blender_result, out_whole, preferred_element_type=jnp.float32).astype(jnp.bfloat16),
        "exp",
        scatter_dimension=0,
        tiled=True,
    ).astype(jnp.float32)
    residual = (own_tokens.astype(jnp.float32) + projected).astype(jnp.bfloat16)
    stream = residual.astype(jnp.float32)
    normed = (
        stream
        * lax.rsqrt(jnp.mean(stream * stream, -1, keepdims=True) + 1e-05)
        * norm_gain[None, :]
    ).astype(jnp.bfloat16)
    logits = jnp.dot(normed, router_weight, preferred_element_type=jnp.float32)
    experts = router_weight.shape[1]
    expert_range = jnp.arange(experts, dtype=jnp.int32)
    chosen = expert_ids[:, :, None] == expert_range[None, None, :]
    selected_entry = jnp.sum(jnp.where(chosen, logits[:, None, :], 0.0), -1)
    shares = jax.nn.sigmoid(selected_entry - selected_entry[:, ::-1])
    flat_hits = chosen.reshape(row_count * TOP, experts).astype(jnp.int32)
    earlier_hits = jnp.cumsum(flat_hits, 0) - flat_hits
    slot_index = jnp.sum(earlier_hits * flat_hits, -1)
    target = expert_ids.reshape(-1) * CAP + slot_index
    placed = target[:, None] == jnp.arange(experts * CAP, dtype=jnp.int32)[None, :]
    placed = placed.reshape(row_count, TOP, experts * CAP)
    selector = jnp.any(placed, 1).astype(jnp.bfloat16)
    outgoing = lax.dot_general(
        selector, normed, (((0,), (0,)), ((), ())), preferred_element_type=jnp.float32
    ).astype(jnp.bfloat16)
    outgoing = outgoing.reshape(experts, CAP, -1)
    arrived = lax.all_to_all(outgoing, "exp", split_axis=0, concat_axis=0, tiled=True)
    arrived = arrived.reshape(-1, arrived.shape[2])
    gate_part = expert_gate[0]
    up_part = expert_up[0]
    down_part = expert_down[0]
    shard_rows = lax.all_gather(arrived, "ctx", axis=0, tiled=True)
    gate_value = lax.dot_general(
        shard_rows, gate_part, (((1,), (1,)), ((), ())), preferred_element_type=jnp.float32
    )
    up_value = lax.dot_general(
        shard_rows, up_part, (((1,), (1,)), ((), ())), preferred_element_type=jnp.float32
    )
    hidden = (jax.nn.silu(gate_value) * up_value).astype(jnp.bfloat16)
    partial_out = jnp.dot(hidden, down_part, preferred_element_type=jnp.float32)
    finished = lax.psum_scatter(
        partial_out.astype(jnp.bfloat16), "ctx", scatter_dimension=0, tiled=True
    )
    returned = lax.all_to_all(
        finished.reshape(experts, CAP, -1), "exp", split_axis=0, concat_axis=0, tiled=True
    )
    returned = returned.reshape(experts * CAP, -1).astype(jnp.float32)
    combine = jnp.sum(jnp.where(placed, shares[:, :, None], 0.0), 1)
    moe_out = jnp.dot(combine, returned, precision=precise)
    return (stream + moe_out).astype(jnp.bfloat16)


def solution(mesh):
    in_specs = (
        P("ctx", "exp"),
        P("ctx", "exp"),
        P("ctx", "exp"),
        P(None, "exp"),
        P("exp"),
        P("exp", None),
        P("ctx", "exp"),
        P("exp"),
        P("exp", "ctx"),
        P(),
        P(),
        P("exp", "ctx", None),
        P("exp", "ctx", None),
        P("exp", "ctx", None),
        P(("ctx", "exp"), None),
    )
    out_specs = P(("ctx", "exp"), None)
    return jax.shard_map(local, mesh=mesh, in_specs=in_specs, out_specs=out_specs, check_vma=False)
```

profile of v0, /device:TPU:0, one launch (start us, length us, event | category | flops | bytes accessed | tf_op | source)
XLA Modules:
  0.0 431.0 jit_solution(18295320063830288196)
XLA Ops:
  6.5 0.7 all-gather.5.cloned.1.call-update
  7.3 0.7 all-gather.7.cloned.1.call-update
  8.1 0.7 all-gather.9.cloned.1.call-update
  8.8 0.5 all-gather.11.cloned.1.call-update
  9.4 0.9 fusion.65
  10.3 1.2 reduce_window_sum.22
  11.5 37.6 %all-gather.5.cloned.1.call-done = bf16[128,4096]{1,0:T(8,128)(2,1)} async-done(((bf16[128,256]{1,0:T(8,128)(2,1)}), bf16[128,4096]{1,0:T(8,128)(2,1)}) %all-gather.5.cloned.1.call-update) | async-done | bytes 1048592 | tf_op jit(solution)/shard_map/all_gather | solution.py:46
  49.1 57.8 %all-gather.7.cloned.1.call-done = bf16[4096,512]{1,0:T(8,128)(2,1)} async-done(((bf16[2048,512]{1,0:T(8,128)(2,1)}), bf16[4096,512]{1,0:T(8,128)(2,1)}) %all-gather.7.cloned.1.call-update) | async-done | bytes 4194320 | tf_op jit(solution)/shard_map/all_gather | solution.py:51
  106.9 3.2 convolution_convert_fusion.3
  110.1 2.2 collective-permute-start
  112.4 52.9 %all-gather.9.cloned.1.call-done = bf16[4096,512]{1,0:T(8,128)(2,1)} async-done(((bf16[2048,512]{1,0:T(8,128)(2,1)}), bf16[4096,512]{1,0:T(8,128)(2,1)}) %all-gather.9.cloned.1.call-update) | async-done | bytes 4194320 | tf_op jit(solution)/shard_map/all_gather | solution.py:56
  165.2 3.2 fusion.36
  168.8 61.2 %psum.7 = f32[128,32]{0,1:T(8,128)S(1)} all-reduce(f32[128,32]{0,1:T(8,128)S(1)} %fusion.66), channel_id=1, replica_groups=mesh['ctx'=2,'exp'=16] {'exp'}, use_global_device_ids=true, to_apply=%region_1.2 | all-reduce | flops 4096 | bytes 32768 | tf_op jit(solution)/shard_map/psum | solution.py:70
  230.6 2.5 collective-permute-start.1
  233.2 39.0 %while.2 = (s32[]{:T(128)}, f32[4,128,128]{2,1,0:T(8,128)S(1)}, f32[4,128,128]{2,1,0:T(8,128)S(1)}, f32[4,128,128]{2,1,0:T(8,128)S(1)}, f32[128,128]{1,0:T(8,128)S(1)}, /*index=5*/s32[]{:T(128)}) while((s32[]{:T(128)}, f32[4,128,128]{2,1,0:T(8,128)S(1)}, f32[4,128,128]{2,1,0:T(8,128)S(1)}, f32[4,128,128]{2,1,0:T(8,128)S(1)}, ...), condition=%wide.region_3.4_spmd, body=%wide.region_2.3_spmd.sunk | while | flops 35667968 | bytes 688205 | solution.py:81
  233.2 9.7 %fusion.90 = f32[128,1,128]{2,1,0:T(1,128)S(1)} fusion(f32[128,128,1]{1,2,0:T(1,128)S(1)} %bitcast.83, f32[128,128]{1,0:T(8,128)S(1)} %get-tuple-element.100, f32[128,128]{1,0:T(8,128)S(1)} %get-tuple-element.101, pred[128,128]{1,0:T(8,128)(4,1)S(1)} %iota_compare_fusion.5), kind=kOutput, calls=%fused_computation.clone.1 | convolution fusion | flops 35651584 | bytes 278528 | tf_op jit(solution)/shard_map/while/body/eval_jaxpr/ts,tsc,sc->tc/dot_general | solution.py:26
  243.0 9.7 %fusion.90 = f32[128,1,128]{2,1,0:T(1,128)S(1)} fusion(f32[128,128,1]{1,2,0:T(1,128)S(1)} %bitcast.83, f32[128,128]{1,0:T(8,128)S(1)} %get-tuple-element.100, f32[128,128]{1,0:T(8,128)S(1)} %get-tuple-element.101, pred[128,128]{1,0:T(8,128)(4,1)S(1)} %iota_compare_fusion.5), kind=kOutput, calls=%fused_computation.clone.1 | convolution fusion | flops 35651584 | bytes 278528 | tf_op jit(solution)/shard_map/while/body/eval_jaxpr/ts,tsc,sc->tc/dot_general | solution.py:26
  252.7 9.7 %fusion.90 = f32[128,1,128]{2,1,0:T(1,128)S(1)} fusion(f32[128,128,1]{1,2,0:T(1,128)S(1)} %bitcast.83, f32[128,128]{1,0:T(8,128)S(1)} %get-tuple-element.100, f32[128,128]{1,0:T(8,128)S(1)} %get-tuple-element.101, pred[128,128]{1,0:T(8,128)(4,1)S(1)} %iota_compare_fusion.5), kind=kOutput, calls=%fused_computation.clone.1 | convolution fusion | flops 35651584 | bytes 278528 | tf_op jit(solution)/shard_map/while/body/eval_jaxpr/ts,tsc,sc->tc/dot_general | solution.py:26
  262.5 9.7 %fusion.90 = f32[128,1,128]{2,1,0:T(1,128)S(1)} fusion(f32[128,128,1]{1,2,0:T(1,128)S(1)} %bitcast.83, f32[128,128]{1,0:T(8,128)S(1)} %get-tuple-element.100, f32[128,128]{1,0:T(8,128)S(1)} %get-tuple-element.101, pred[128,128]{1,0:T(8,128)(4,1)S(1)} %iota_compare_fusion.5), kind=kOutput, calls=%fused_computation.clone.1 | convolution fusion | flops 35651584 | bytes 278528 | tf_op jit(solution)/shard_map/while/body/eval_jaxpr/ts,tsc,sc->tc/dot_general | solution.py:26
  272.2 0.5 fusion.35
  272.8 3.9 convolution_convert_fusion
  277.4 52.7 %reduce-scatter.3.cloned.1.call-done = bf16[8,4096]{1,0:T(8,128)(2,1)} async-done(((bf16[128,4096]{1,0:T(8,128)(2,1)}), bf16[8,4096]{1,0:T(8,128)(2,1)}) %reduce-scatter.3.cloned.1.call-update) | async-done | bytes 65552 | tf_op jit(solution)/shard_map/reduce_scatter | solution.py:104
  330.1 1.0 fusion.50
  331.7 13.5 %all_to_all.10 = bf16[16,2,4096]{2,1,0:T(2,128)(2,1)S(1)} all-to-all(bf16[16,2,4096]{2,1,0:T(2,128)(2,1)S(1)} %reshape.79), channel_id=1, replica_groups=mesh['ctx'=2,'exp'=16] {'exp'}, dimensions={0} | all-to-all | bytes 524288 | tf_op jit(solution)/shard_map/all_to_all | solution.py:134
  345.3 8.9 %all_gather.19 = bf16[64,4096]{1,0:T(8,128)(2,1)S(1)} all-gather(bf16[32,4096]{1,0:T(8,128)(2,1)S(1)} %reshape.80), channel_id=1, replica_groups=mesh['ctx'=2,'exp'=16] {'ctx'}, dimensions={0}, use_global_device_ids=true | all-gather | bytes 786432 | tf_op jit(solution)/shard_map/all_gather | solution.py:139
  354.2 14.3 %fusion.18 = f32[64,3584]{1,0:T(8,128)S(1)} fusion(bf16[64,4096]{1,0:T(8,128)(2,1)S(1)} %all_gather.19, bf16[1,3584,4096]{2,1,0:T(8,128)(2,1)} %param.28), kind=kOutput, calls=%fused_computation.22 | convolution fusion | flops 1879048192 | bytes 30801920 | tf_op jit(solution)/shard_map/dot_general | solution.py:140
  368.5 23.9 %fusion.26 = bf16[64,4096]{1,0:T(8,128)(2,1)} fusion(bf16[1,3584,4096]{2,1,0:T(8,128)(2,1)} %param.30, bf16[64,4096]{1,0:T(8,128)(2,1)S(1)} %all_gather.19, bf16[1,3584,4096]{2,1,0:T(8,128)(2,1)} %param.29, f32[64,3584]{1,0:T(8,128)S(1)} %fusion.18), kind=kOutput, calls=%fused_computation.27 | convolution fusion | flops 3759734784 | bytes 60686336 | tf_op jit(solution)/shard_map/dot_general | solution.py:147
  392.4 13.2 %reduce-scatter.5.cloned.1.call-done = bf16[32,4096]{1,0:T(8,128)(2,1)} async-done(((bf16[64,4096]{1,0:T(8,128)(2,1)}), bf16[32,4096]{1,0:T(8,128)(2,1)}) %reduce-scatter.5.cloned.1.call-update) | async-done | bytes 262160 | tf_op jit(solution)/shard_map/reduce_scatter | solution.py:148
  405.7 1.8 reshape.81
  407.5 5.6 %all-to-all-start.1 = ((bf16[16,2,4096]{2,1,0:T(2,128)(2,1)}), bf16[16,2,4096]{2,1,0:T(2,128)(2,1)S(1)}, u32[]{:S(2)}, u32[]{:S(2)}) async-start(bf16[16,2,4096]{2,1,0:T(2,128)(2,1)} %reshape.81), calls=%async_computation.3 | async-start | bytes 524288 | tf_op jit(solution)/shard_map/all_to_all | solution.py:151
  413.6 9.5 %all-to-all-done.1 = bf16[16,2,4096]{2,1,0:T(2,128)(2,1)S(1)} async-done(((bf16[16,2,4096]{2,1,0:T(2,128)(2,1)}), bf16[16,2,4096]{2,1,0:T(2,128)(2,1)S(1)}, u32[]{:S(2)}, u32[]{:S(2)}) %all-to-all-start.1) | async-done | bytes 262176 | tf_op jit(solution)/shard_map/all_to_all | solution.py:151
  423.3 0.9 fusion.29
  (64 shorter events, 3.3 us)
Async XLA Ops:
  6.5 406.6 %copy-start = (bf16[4096,16]{0,1:T(8,128)(2,1)S(1)}, bf16[4096,16]{0,1:T(8,128)(2,1)}, u32[]{:S(2)}) copy-start(bf16[4096,16]{0,1:T(8,128)(2,1)} %param.27) | copy-start | bytes 393220
  6.5 42.5 %all-gather.5.cloned.1.call-start = ((), (), s32[]{:S(2)}) async-start(), calls=%async_computation.4 | async-start | bytes 1114112 | tf_op jit(solution)/shard_map/all_gather | solution.py:46
  7.3 99.6 %all-gather.7.cloned.1.call-start = ((), (), s32[]{:S(2)}) async-start(), calls=%async_computation.5 | async-start | bytes 6291456 | tf_op jit(solution)/shard_map/all_gather | solution.py:51
  8.0 160.5 %copy-start.4 = (f32[512]{0:T(512)S(1)}, f32[512]{0:T(512)}, u32[]{:S(2)}) copy-start(f32[512]{0:T(512)} %param.21) | copy-start | bytes 6148
  8.0 160.7 %copy-start.1 = (bf16[512,32]{0,1:T(8,128)(2,1)S(1)}, bf16[512,32]{0,1:T(8,128)(2,1)}, u32[]{:S(2)}) copy-start(bf16[512,32]{0,1:T(8,128)(2,1)} %param.22) | copy-start | bytes 98308
  8.0 157.2 %all-gather.9.cloned.1.call-start = ((), (), s32[]{:S(2)}) async-start(), calls=%async_computation.6 | async-start | bytes 6291456 | tf_op jit(solution)/shard_map/all_gather | solution.py:56
  8.8 264.0 %all-gather.11.cloned.1.call-start = ((), (), s32[]{:S(2)}) async-start(), calls=%async_computation.7 | async-start | bytes 6291456 | tf_op jit(solution)/shard_map/all_gather | solution.py:103
  9.3 320.8 %reduce-scatter.3.cloned.1.call-start = ((), (), s32[]{:S(2)}) async-start(), calls=%async_computation.8 | async-start | bytes 1114112 | tf_op jit(solution)/shard_map/reduce_scatter | solution.py:104
  110.1 58.3 %collective-permute-start = (bf16[3,512]{1,0:T(4,128)(2,1)S(1)}, bf16[3,512]{1,0:T(4,128)(2,1)S(1)}, u32[]{:S(2)}, u32[]{:S(2)}) collective-permute-start(bf16[3,512]{1,0:T(4,128)(2,1)S(1)} %slice.48), channel_id=1, source_target_pairs={{0,16},{1,17},{2,18},{3,19},{4,20},{5,21},{6,22},{7,23},{8,24},{9,... | collective-permute-start | bytes 9224 | tf_op jit(solution)/shard_map/ppermute | solution.py:18
  230.6 41.6 %collective-permute-start.1 = (f32[512,16]{0,1:T(8,128)S(1)}, f32[512,16]{0,1:T(8,128)S(1)}, u32[]{:S(2)}, u32[]{:S(2)}) collective-permute-start(f32[512,16]{0,1:T(8,128)S(1)} %convolution_add_fusion.1), channel_id=1, source_target_pairs={{0,16},{1,17},{2,18},{3,19},{4,20},{5,21},{6,22},{7,23},{8,24},{9,... | collective-permute-start | bytes 98312 | tf_op jit(solution)/shard_map/while/body/eval_jaxpr/ppermute | solution.py:18
  233.1 39.1 %copy-start.5 = (f32[512]{0:T(512)S(1)}, f32[512]{0:T(512)}, u32[]{:S(2)}) copy-start(f32[512]{0:T(512)} %param.24) | copy-start | bytes 6148
  233.2 43.6 %copy-start.3 = (s32[8,2]{0,1:T(2,128)S(1)}, s32[8,2]{0,1:T(2,128)}, u32[]{:S(2)}) copy-start(s32[8,2]{0,1:T(2,128)} %param.31) | copy-start | bytes 196
  272.2 59.0 %copy-start.2 = (f32[4096]{0:T(1024)S(1)}, f32[4096]{0:T(1024)}, u32[]{:S(2)}) copy-start(f32[4096]{0:T(1024)} %param.26) | copy-start | bytes 49156
  276.7 129.0 %reduce-scatter.5.cloned.1.call-start = ((), (), s32[]{:S(2)}) async-start(), calls=%async_computation.9 | async-start | bytes 786432 | tf_op jit(solution)/shard_map/reduce_scatter | solution.py:148
  407.5 15.7 %all-to-all-start.1 = ((bf16[16,2,4096]{2,1,0:T(2,128)(2,1)}), bf16[16,2,4096]{2,1,0:T(2,128)(2,1)S(1)}, u32[]{:S(2)}, u32[]{:S(2)}) async-start(bf16[16,2,4096]{2,1,0:T(2,128)(2,1)} %reshape.81), calls=%async_computation.3 | async-start | bytes 524288 | tf_op jit(solution)/shard_map/all_to_all | solution.py:151
Sparse Core Ops, SparseCore 0:
  9.5 39.4 all-gather.4
  50.6 56.2 all-gather.6
  108.4 56.7 all-gather.8
  166.6 56.7 all-gather.10
  276.8 53.3 reduce-scatter.2
  392.5 13.0 reduce-scatter.4
where the time goes:
time: 431 us
  waiting for transfers between devices  226 us (52%)
  matrix products  89.8 us (21%)
  blocking collectives  83.7 us (19%)
  between operations  13.7 us (3%)
  starting transfers between devices  10.5 us (2%)
    psum x1, blocking collectives, local(): lax.psum(jnp.dot(mixer_in, state_weight, preferred_element_type=jnp.float...  61.2 us
    all_gather x1, waiting for transfers between devices, local(): lax.all_gather(input_weight, 'ctx', axis=0, tiled=True)  57.8 us
    all_gather x1, waiting for transfers between devices, local(): lax.all_gather(gate_weight, 'ctx', axis=0, tiled=True)  52.9 us
    reduce_scatter x1, waiting for transfers between devices, local(): lax.psum_scatter(jnp.dot(blender_result, out_whole, preferred_element_typ...  52.7 us
    dot_general x4, matrix products, causal_part(): jnp.einsum('ts,tsc,sc->tc', scores, weight, input_block, precision=precise)  38.7 us
    all_gather x1, waiting for transfers between devices, local(): whole_stretch = lax.all_gather(tokens, 'exp', axis=1, tiled=True)  37.6 us
    dot_general x1, matrix products, local(): partial_out = jnp.dot(hidden, down_part, preferred_element_type=jnp.float32)  23.9 us
    dot_general x1, matrix products, local(): lax.dot_general(shard_rows, gate_part, (((1,), (1,)), ((), ())), preferre...  14.3 us
  transfers between devices with their start and end apart: 9, of which 6 were waited for; matrix products, arithmetic and copies ran while one was open for 12% of the time, Pallas kernels for 0%

commit v1 on v0

v1 whole, which is shorter than its diff:
```python
import jax
import jax.numpy as jnp
from jax import lax
from jax.experimental import pallas as pl
from jax.experimental.pallas import tpu as pltpu
from jax.sharding import PartitionSpec as P

STATE = 16
CONV = 4
TOP = 2
CAP = 2
CHUNK = 64

precise = lax.Precision.HIGHEST
f32 = jnp.float32
bf16 = jnp.bfloat16


def partner(shard, axis, mask):
    devices = lax.axis_size(axis)
    return lax.ppermute(shard, axis, [(i, i ^ mask) for i in range(devices)])


def gather_bit(shard, axis, mask):
    other = partner(shard, axis, mask)
    high = (lax.axis_index(axis) & mask) != 0
    return jnp.stack([jnp.where(high, other, shard), jnp.where(high, shard, other)], 0)


def swap(pieces, axis):
    if lax.axis_size(axis) != 2:
        return lax.all_to_all(pieces, axis, split_axis=0, concat_axis=0, tiled=True)
    me = lax.axis_index(axis)
    own = lax.dynamic_index_in_dim(pieces, me, 0, keepdims=False)
    other = partner(lax.dynamic_index_in_dim(pieces, 1 - me, 0, keepdims=False), axis, 1)
    return jnp.stack([jnp.where(me == 0, own, other), jnp.where(me == 0, other, own)], 0)


def swap_sum(pieces, axis):
    if lax.axis_size(axis) != 2:
        got = lax.all_to_all(pieces.astype(bf16), axis, split_axis=0, concat_axis=0, tiled=True)
        return jnp.sum(got.astype(f32), 0)
    me = lax.axis_index(axis)
    own = lax.dynamic_index_in_dim(pieces, me, 0, keepdims=False)
    leaving = lax.dynamic_index_in_dim(pieces, 1 - me, 0, keepdims=False).astype(bf16)
    return own.astype(f32) + partner(leaving, axis, 1).astype(f32)


def gather_ctx(shard):
    if lax.axis_size("ctx") == 2:
        return gather_bit(shard, "ctx", 1)
    return lax.all_gather(shard, "ctx", axis=0)


def sum_all(value):
    for mask in [1 << b for b in range(lax.axis_size("exp").bit_length() - 1)]:
        value = value + partner(value, "exp", mask)
    for mask in [1 << b for b in range(lax.axis_size("ctx").bit_length() - 1)]:
        value = value + partner(value, "ctx", mask)
    return value


def scan_kernel(mixer_ref, gate_ref, proj_ref, step_ref, skip_ref, out_ref):
    tokens, width = mixer_ref.shape
    chunk = min(CHUNK, tokens)
    rows = lax.broadcasted_iota(jnp.int32, (chunk, chunk), 0)
    columns = lax.broadcasted_iota(jnp.int32, (chunk, chunk), 1)
    causal = rows >= columns
    ones = causal.astype(f32)

    def dot(a, b, dims):
        return lax.dot_general(a, b, (dims, ((), ())), precision=precise, preferred_element_type=f32)

    state = jnp.zeros((STATE, width), f32)
    for start in range(0, tokens, chunk):
        at = pl.ds(start, chunk)
        decay = dot(ones, step_ref[at, :], ((1,), (0,)))
        half = 0.5 * decay[chunk - 1 : chunk, :]
        mixer = mixer_ref[at, :].astype(f32)
        raised = mixer * jnp.exp(decay - half)
        gain = proj_ref[at, :STATE]
        read = proj_ref[at, STATE:]
        scores = jnp.where(causal, dot(read, gain, ((1,), (1,))), 0.0)
        fall = jnp.exp(-half)
        state = state * fall
        reading = jnp.exp(half - decay) * (
            dot(scores, raised, ((1,), (0,))) + dot(read, state, ((1,), (0,)))
        )
        state = fall * (state + dot(gain, raised, ((0,), (0,))))
        gate = gate_ref[at, :].astype(f32)
        mixed = (reading + skip_ref[...] * mixer) * (gate * jax.nn.sigmoid(gate))
        out_ref[at, :] = mixed.astype(out_ref.dtype)


def local(
    tokens,
    input_weight,
    gate_weight,
    conv_weight,
    conv_bias,
    state_weight,
    step_size,
    skip_gain,
    output_weight,
    norm_gain,
    router_weight,
    expert_gate,
    expert_up,
    expert_down,
    expert_ids,
):
    nx, ne = lax.axis_size("ctx"), lax.axis_size("exp")
    ctx, exp = lax.axis_index("ctx"), lax.axis_index("exp")
    stretch, part = tokens.shape
    total = stretch * nx
    rows = expert_ids.shape[0]
    width = input_weight.shape[1] // nx

    masks = [1 << b for b in range(ne.bit_length() - 1)]
    outer_bits = max(2, nx.bit_length() - 1)
    inner_masks, outer_masks = masks[: len(masks) - outer_bits], masks[len(masks) - outer_bits :]
    block = tokens
    for mask in outer_masks:
        block = gather_bit(block, "exp", mask)
    outer = 1 << outer_bits
    block = block.reshape(nx, outer // nx, stretch, part)
    block = swap(block, "ctx")
    for mask in reversed(inner_masks):
        block = gather_bit(block, "exp", mask)
    inner = 1 << len(inner_masks)
    lead = len(inner_masks)
    block = block.reshape((2,) * lead + (nx, outer // nx, stretch, part))
    order = (lead, lead + 2, lead + 1) + tuple(reversed(range(lead))) + (lead + 3,)
    everything = block.transpose(order).reshape(total, outer // nx * inner * part)

    inner_x = jnp.dot(everything, input_weight, preferred_element_type=f32)
    inner_x = inner_x.reshape(total, nx, width).transpose(1, 0, 2)
    inner_x = swap_sum(inner_x, "ctx").astype(bf16)
    inner_z = jnp.dot(everything, gate_weight, preferred_element_type=f32)
    inner_z = inner_z.reshape(total, nx, width).transpose(1, 0, 2)
    inner_z = swap_sum(inner_z, "ctx").astype(bf16)

    def mine(array, axis):
        return lax.dynamic_slice_in_dim(array, ctx * width, width, axis)

    extended = jnp.pad(inner_x, ((CONV - 1, 0), (0, 0))).astype(f32)
    taps = mine(conv_weight, 1)
    filtered = jnp.broadcast_to(mine(conv_bias, 0)[None, :], (total, width))
    for offset in range(CONV):
        filtered = filtered + taps[offset][None, :] * extended[offset : offset + total]
    mixer_in = jax.nn.silu(filtered).astype(bf16)
    projections = sum_all(
        jnp.dot(mixer_in, mine(state_weight, 0), preferred_element_type=f32)
    )
    steps = swap(step_size.reshape(stretch, nx, width).transpose(1, 0, 2), "ctx")
    steps = steps.reshape(total, width)
    mixer_out = pl.pallas_call(
        scan_kernel,
        out_shape=jax.ShapeDtypeStruct((total, width), bf16),
        in_specs=[pl.BlockSpec(memory_space=pltpu.VMEM)] * 5,
        out_specs=pl.BlockSpec(memory_space=pltpu.VMEM),
        compiler_params=pltpu.CompilerParams(vmem_limit_bytes=32 * 1024 * 1024),
        name="state_scan",
    )(mixer_in, inner_z, projections, steps, mine(skip_gain, 0)[None, :])

    mixer_out = gather_ctx(mixer_out).transpose(1, 0, 2).reshape(total, nx * width)
    partial = jnp.dot(mixer_out, output_weight, preferred_element_type=f32).astype(bf16)
    columns = partial.shape[1]
    partial = partial.reshape(nx, ne // 2, 2, rows, columns).transpose(2, 1, 0, 3, 4)
    low = exp & 1
    own = lax.dynamic_index_in_dim(partial, low, 0, keepdims=False).astype(f32)
    other = partner(lax.dynamic_index_in_dim(partial, 1 - low, 0, keepdims=False), "exp", 1)
    pair = (own + other.astype(f32)).astype(bf16)
    groups = [[2 * i + k for i in range(ne // 2)] for k in range(2)]
    pieces = lax.all_to_all(
        pair, "exp", split_axis=0, concat_axis=0, tiled=True, axis_index_groups=groups
    )
    projected = jnp.sum(pieces.astype(f32), 0)
    own_tokens = lax.dynamic_index_in_dim(
        everything.reshape(nx, ne, rows, columns), exp, 1, keepdims=False
    )
    residual = (own_tokens.astype(f32) + projected).astype(bf16)

    experts = router_weight.shape[1]
    everyone = gather_ctx(expert_ids)
    chosen = (everyone[..., None] == jnp.arange(experts, dtype=jnp.int32)).astype(jnp.int32)
    hits = chosen.reshape(nx, rows * TOP, experts)
    earlier = jnp.cumsum(hits, 1) - hits
    slot = jnp.sum(earlier * hits, -1).reshape(nx, rows, TOP)
    place = everyone * CAP + slot
    placed = place[..., None] == jnp.arange(experts * CAP, dtype=jnp.int32)
    selector = jnp.any(placed, 2).astype(bf16)
    outgoing = lax.dot_general(
        selector, residual, (((1,), (1,)), ((0,), (0,))), preferred_element_type=f32
    ).astype(bf16)
    outgoing = outgoing.reshape(nx, experts, CAP, columns).transpose(1, 0, 2, 3)
    outgoing = jnp.broadcast_to(outgoing[None], (nx,) + outgoing.shape)
    outgoing = outgoing.reshape(nx * experts, nx * CAP, columns)
    arrived = lax.all_to_all(outgoing, ("ctx", "exp"), split_axis=0, concat_axis=0, tiled=True)
    slots = experts * nx * CAP
    arrived = arrived.reshape(nx, slots, columns).transpose(1, 0, 2).reshape(slots, nx * columns)

    def norm(values):
        wide = values.astype(f32)
        scale = lax.rsqrt(jnp.mean(wide * wide, -1, keepdims=True) + 1e-05)
        return (wide * scale * norm_gain[None, :]).astype(bf16)

    normed = norm(arrived)
    gate_value = lax.dot_general(
        normed, expert_gate[0], (((1,), (1,)), ((), ())), preferred_element_type=f32
    )
    up_value = lax.dot_general(
        normed, expert_up[0], (((1,), (1,)), ((), ())), preferred_element_type=f32
    )
    hidden = (jax.nn.silu(gate_value) * up_value).astype(bf16)
    finished = jnp.dot(hidden, expert_down[0], preferred_element_type=f32).astype(bf16)
    finished = finished.reshape(experts, nx, CAP, -1).transpose(1, 0, 2, 3)
    finished = finished.reshape(nx * experts, CAP, -1)
    returned = lax.all_to_all(finished, ("ctx", "exp"), split_axis=0, concat_axis=0, tiled=True)
    returned = returned.reshape(nx, experts * CAP, -1)
    returned = jnp.sum(returned.astype(f32), 0)

    home = swap(residual, "ctx").transpose(1, 0, 2).reshape(rows, nx * columns)
    logits = jnp.dot(norm(home), router_weight, preferred_element_type=f32)
    my_choice = expert_ids[:, :, None] == jnp.arange(experts, dtype=jnp.int32)
    picked = jnp.sum(jnp.where(my_choice, logits[:, None, :], 0.0), -1)
    shares = jax.nn.sigmoid(picked - picked[:, ::-1])
    my_placed = lax.dynamic_index_in_dim(placed, ctx, 0, keepdims=False)
    combine = jnp.sum(jnp.where(my_placed, shares[:, :, None], 0.0), 1)
    moe_out = jnp.dot(combine, returned, precision=precise)
    return (home.astype(f32) + moe_out).astype(bf16)


def solution(mesh):
    in_specs = (
        P("ctx", "exp"),
        P("ctx", "exp"),
        P("ctx", "exp"),
        P(None, "exp"),
        P("exp"),
        P("exp", None),
        P("ctx", "exp"),
        P("exp"),
        P("exp", "ctx"),
        P(),
        P(),
        P("exp", "ctx", None),
        P("exp", "ctx", None),
        P("exp", "ctx", None),
        P(("ctx", "exp"), None),
    )
    out_specs = P(("ctx", "exp"), None)
    return jax.shard_map(local, mesh=mesh, in_specs=in_specs, out_specs=out_specs, check_vma=False)
```

time: 431 us -> 192 us (0.45)
  waiting for transfers between devices: 226 us -> 76.1 us
  blocking collectives: 83.7 us -> 0 us
  matrix products: 89.8 us -> 46.5 us
  starting transfers between devices: 10.5 us -> 37.1 us
  local copies, waits for them, and re-layouts: 3.59 us -> 22.3 us
  between operations: 13.7 us -> 0.47 us
  other arithmetic: 3.16 us -> 7.73 us
    all_gather x4 -> x0, waiting for transfers between devices: 148 us -> none  [the longest x1 57.8 us: local(): lax.all_gather(input_weight, 'ctx', axis=0, tiled=True)]
    reduce_scatter x2 -> x0, waiting for transfers between devices: 65.9 us -> none  [the longest x1 52.7 us: local(): lax.psum_scatter(jnp.dot(blender_result, out_whole, preferred_element_typ...]
    psum x1 -> x0, blocking collectives: 61.2 us -> none  [local(): lax.psum(jnp.dot(mixer_in, state_weight, preferred_element_type=jnp.float...]
    dot_general x15 -> x8, matrix products: 88.9 us -> 44.5 us  [the longest x1 23.1 us: local(): jnp.dot(hidden, expert_down[0], preferred_element_type=f32).astype(bf16)]
    ppermute x2 -> x17, waiting for transfers between devices: 0.01 us -> 38 us  [partner(): return lax.ppermute(shard, axis, [(i, i ^ mask) for i in range(devices)])]
    all_to_all x1 -> x3, waiting for transfers between devices: 9.55 us -> 38.1 us  [the longest x1 15.3 us: local(): lax.all_to_all(finished, ('ctx', 'exp'), split_axis=0, concat_axis=0, til...]
    ppermute x2 -> x17, starting transfers between devices: 4.68 us -> 24.2 us  [partner(): return lax.ppermute(shard, axis, [(i, i ^ mask) for i in range(devices)])]
    all_to_all x1 -> x0, blocking collectives: 13.5 us -> none  [local(): lax.all_to_all(outgoing, 'exp', split_axis=0, concat_axis=0, tiled=True)]
  transfers between devices with their start and end apart: 9 -> 20, of which waited for: 6 -> 13; matrix products, arithmetic and copies ran while one was open for 12% -> 10% of each run, Pallas kernels for 0% -> 0%
where the time goes in v1:
time: 192 us
  waiting for transfers between devices  76.1 us (40%)
  matrix products  46.5 us (24%)
  starting transfers between devices  37.1 us (19%)
  local copies, waits for them, and re-layouts  22.3 us (12%)
  other arithmetic  7.73 us (4%)
    ppermute x17, waiting for transfers between devices, partner(): return lax.ppermute(shard, axis, [(i, i ^ mask) for i in range(devices)])  38 us
    ppermute x17, starting transfers between devices, partner(): return lax.ppermute(shard, axis, [(i, i ^ mask) for i in range(devices)])  24.2 us
    dot_general x1, matrix products, local(): jnp.dot(hidden, expert_down[0], preferred_element_type=f32).astype(bf16)  23.1 us
    all_to_all x1, waiting for transfers between devices, local(): lax.all_to_all(finished, ('ctx', 'exp'), split_axis=0, concat_axis=0, til...  15.3 us
    dot_general x1, matrix products, local(): lax.dot_general(normed, expert_gate[0], (((1,), (1,)), ((), ())), preferr...  14.3 us
    all_to_all x1, waiting for transfers between devices, local(): lax.all_to_all(pair, 'exp', split_axis=0, concat_axis=0, tiled=True, axis...  13 us
    all_to_all x1, waiting for transfers between devices, local(): lax.all_to_all(outgoing, ('ctx', 'exp'), split_axis=0, concat_axis=0, til...  9.74 us
    all_to_all x1, starting transfers between devices, local(): lax.all_to_all(pair, 'exp', split_axis=0, concat_axis=0, tiled=True, axis...  5.73 us
  transfers between devices with their start and end apart: 20, of which 13 were waited for; matrix products, arithmetic and copies ran while one was open for 10% of the time, Pallas kernels for 0%

profile of v1, /device:TPU:0, one launch (start us, length us, event | category | flops | bytes accessed | tf_op | source)
XLA Modules:
  0.0 191.7 jit_solution(6052544250141352864)
XLA Ops:
  0.0 3.0 %collective-permute-start = (bf16[128,256]{1,0:T(8,128)(2,1)}, bf16[128,256]{1,0:T(8,128)(2,1)S(1)}, u32[]{:S(2)}, u32[]{:S(2)}) collective-permute-start(bf16[128,256]{1,0:T(8,128)(2,1)} %param.15), channel_id=1, source_target_pairs={{0,4},{1,5},{2,6},{3,7},{4,0},{5,1},{6,2},{7,3},{8,12},{9,13},{10,... | collective-permute-start | bytes 196616 | tf_op jit(solution)/shard_map/ppermute | solution.py:21
  3.0 2.5 %collective-permute-done = bf16[128,256]{1,0:T(8,128)(2,1)S(1)} collective-permute-done((bf16[128,256]{1,0:T(8,128)(2,1)}, bf16[128,256]{1,0:T(8,128)(2,1)S(1)}, u32[]{:S(2)}, u32[]{:S(2)}) %collective-permute-start) | collective-permute-done | bytes 65568 | tf_op jit(solution)/shard_map/ppermute | solution.py:21
  6.4 3.1 %collective-permute-start.1 = (bf16[2,128,256]{2,1,0:T(8,128)(2,1)S(1)}, bf16[2,128,256]{2,1,0:T(8,128)(2,1)S(1)}, u32[]{:S(2)}, u32[]{:S(2)}) collective-permute-start(bf16[2,128,256]{2,1,0:T(8,128)(2,1)S(1)} %pad_maximum_fusion.3), channel_id=1, source_target_pairs={{0,8},{1,9},{2,10},{3,11},{4,12},{5,13},{6,14},{7,15},{8,0},{9,1},... | collective-permute-start | bytes 393224 | tf_op jit(solution)/shard_map/ppermute | solution.py:21
  9.5 5.2 %collective-permute-done.1 = bf16[2,128,256]{2,1,0:T(8,128)(2,1)S(1)} collective-permute-done((bf16[2,128,256]{2,1,0:T(8,128)(2,1)S(1)}, bf16[2,128,256]{2,1,0:T(8,128)(2,1)S(1)}, u32[]{:S(2)}, u32[]{:S(2)}) %collective-permute-start.1) | collective-permute-done | bytes 131104 | tf_op jit(solution)/shard_map/ppermute | solution.py:21
  14.7 1.6 collective-permute-start.2
  16.3 3.4 %collective-permute-done.2 = bf16[2,128,256]{2,1,0:T(8,128)(2,1)S(1)} collective-permute-done((bf16[2,128,256]{2,1,0:T(8,128)(2,1)S(1)}, bf16[2,128,256]{2,1,0:T(8,128)(2,1)S(1)}, u32[]{:S(2)}, u32[]{:S(2)}) %collective-permute-start.2) | collective-permute-done | bytes 131104 | tf_op jit(solution)/shard_map/ppermute | solution.py:21
  19.9 1.6 collective-permute-start.3
  21.5 4.8 %collective-permute-done.3 = bf16[2,2,128,256]{3,2,1,0:T(8,128)(2,1)S(1)} collective-permute-done((bf16[2,2,128,256]{3,2,1,0:T(8,128)(2,1)S(1)}, bf16[2,2,128,256]{3,2,1,0:T(8,128)(2,1)S(1)}, u32[]{:S(2)}, u32[]{:S(2)}) %collective-permute-start.3) | collective-permute-done | bytes 262176 | tf_op jit(solution)/shard_map/ppermute | solution.py:21
  27.2 4.0 %copy.96 = bf16[512,2048]{1,0:T(8,128)(2,1)} copy(bf16[512,2048]{0,1:T(8,128)(2,1)} %bitcast.152) | data formatting | bytes 4194304 | tf_op jit(solution)/shard_map/dot_general | solution.py:136
  33.5 1.6 reshape.149
  35.2 2.7 %fusion.53 = f32[256,2,256]{2,0,1:T(8,128)S(1)} fusion(bf16[256,2048,1]{1,0,2:T(8,128)(2,1)} %reshape.149, bf16[2,256,2048]{2,1,0:T(8,128)(2,1)} %bitcast.155), kind=kOutput, calls=%fused_computation.113 | convolution fusion | flops 536870912 | bytes 3670016 | tf_op jit(solution)/shard_map/dot_general | solution.py:136
  41.5 4.0 %copy.97 = bf16[512,2048]{1,0:T(8,128)(2,1)} copy(bf16[512,2048]{0,1:T(8,128)(2,1)} %bitcast.153) | data formatting | bytes 4194304 | tf_op jit(solution)/shard_map/dot_general | solution.py:139
  47.4 2.1 %fusion.54 = f32[256,2,256]{2,0,1:T(8,128)S(1)} fusion(bf16[256,2048,1]{1,0,2:T(8,128)(2,1)} %reshape.149, bf16[2,256,2048]{2,1,0:T(8,128)(2,1)S(1)} %bitcast.154), kind=kOutput, calls=%fused_computation.114 | convolution fusion | flops 536870912 | bytes 3670016 | tf_op jit(solution)/shard_map/dot_general | solution.py:139
  49.6 1.6 collective-permute-start.8
  52.8 2.7 %collective-permute-done.8 = f32[256,32]{1,0:T(8,128)S(1)} collective-permute-done((f32[256,32]{1,0:T(8,128)S(1)}, f32[256,32]{1,0:T(8,128)S(1)}, u32[]{:S(2)}, u32[]{:S(2)}) %collective-permute-start.8) | collective-permute-done | bytes 32800 | tf_op jit(solution)/shard_map/ppermute | solution.py:21
  57.9 2.8 %collective-permute-done.9 = f32[256,32]{1,0:T(8,128)S(1)} collective-permute-done((f32[256,32]{1,0:T(8,128)S(1)}, f32[256,32]{1,0:T(8,128)S(1)}, u32[]{:S(2)}, u32[]{:S(2)}) %collective-permute-start.9) | collective-permute-done | bytes 32800 | tf_op jit(solution)/shard_map/ppermute | solution.py:21
  60.8 2.4 %collective-permute-start.10 = (f32[256,32]{1,0:T(8,128)S(1)}, f32[256,32]{1,0:T(8,128)S(1)}, u32[]{:S(2)}, u32[]{:S(2)}) collective-permute-start(f32[256,32]{1,0:T(8,128)S(1)} %add.133), channel_id=1, source_target_pairs={{0,8},{1,9},{2,10},{3,11},{4,12},{5,13},{6,14},{7,15},{8,0},{9,1},... | collective-permute-start | bytes 98312 | tf_op jit(solution)/shard_map/ppermute | solution.py:21
  63.2 5.6 %collective-permute-done.10 = f32[256,32]{1,0:T(8,128)S(1)} collective-permute-done((f32[256,32]{1,0:T(8,128)S(1)}, f32[256,32]{1,0:T(8,128)S(1)}, u32[]{:S(2)}, u32[]{:S(2)}) %collective-permute-start.10) | collective-permute-done | bytes 32800 | tf_op jit(solution)/shard_map/ppermute | solution.py:21
  70.4 3.4 %collective-permute-done.11 = f32[256,32]{1,0:T(8,128)S(1)} collective-permute-done((f32[256,32]{1,0:T(8,128)S(1)}, f32[256,32]{1,0:T(8,128)S(1)}, u32[]{:S(2)}, u32[]{:S(2)}) %collective-permute-start.11) | collective-permute-done | bytes 32800 | tf_op jit(solution)/shard_map/ppermute | solution.py:21
  77.0 3.5 %collective-permute-done.13 = bf16[256,256]{1,0:T(8,128)(2,1)S(1)} collective-permute-done((bf16[256,256]{1,0:T(8,128)(2,1)S(1)}, bf16[256,256]{1,0:T(8,128)(2,1)S(1)}, u32[]{:S(2)}, u32[]{:S(2)}) %collective-permute-start.13) | collective-permute-done | bytes 131104 | tf_op jit(solution)/shard_map/ppermute | solution.py:21
  81.3 1.7 convolution_convert_fusion
  86.1 5.7 %all-to-all-start = ((bf16[8,2,8,2048]{3,2,1,0:T(8,128)(2,1)}), bf16[8,2,8,2048]{3,2,1,0:T(8,128)(2,1)S(1)}, u32[]{:S(2)}, u32[]{:S(2)}) async-start(bf16[8,2,8,2048]{3,2,1,0:T(8,128)(2,1)} %fusion.18), calls=%async_computation | async-start | bytes 1048576 | tf_op jit(solution)/shard_map/all_to_all | solution.py:175
  93.6 13.0 %all-to-all-done = bf16[8,2,8,2048]{3,2,1,0:T(8,128)(2,1)S(1)} async-done(((bf16[8,2,8,2048]{3,2,1,0:T(8,128)(2,1)}), bf16[8,2,8,2048]{3,2,1,0:T(8,128)(2,1)S(1)}, u32[]{:S(2)}, u32[]{:S(2)}) %all-to-all-start) | async-done | bytes 524320 | tf_op jit(solution)/shard_map/all_to_all | solution.py:175
  108.9 3.8 %all-to-all-start.1 = ((bf16[32,4,2048]{2,1,0:T(4,128)(2,1)}), bf16[32,4,2048]{2,1,0:T(4,128)(2,1)S(1)}, u32[]{:S(2)}, u32[]{:S(2)}) async-start(bf16[32,4,2048]{2,1,0:T(4,128)(2,1)} %reshape.141), calls=%async_computation.1 | async-start | bytes 1048576 | tf_op jit(solution)/shard_map/all_to_all | solution.py:199
  112.8 1.7 collective-permute-start.15
  114.4 4.1 %collective-permute-done.15 = bf16[8,2048]{1,0:T(8,128)(2,1)S(1)} collective-permute-done((bf16[8,2048]{1,0:T(8,128)(2,1)S(1)}, bf16[8,2048]{1,0:T(8,128)(2,1)S(1)}, u32[]{:S(2)}, u32[]{:S(2)}) %collective-permute-start.15) | collective-permute-done | bytes 32800 | tf_op jit(solution)/shard_map/ppermute | solution.py:21
  118.7 9.7 %all-to-all-done.1 = bf16[32,4,2048]{2,1,0:T(4,128)(2,1)S(1)} async-done(((bf16[32,4,2048]{2,1,0:T(4,128)(2,1)}), bf16[32,4,2048]{2,1,0:T(4,128)(2,1)S(1)}, u32[]{:S(2)}, u32[]{:S(2)}) %all-to-all-start.1) | async-done | bytes 524320 | tf_op jit(solution)/shard_map/all_to_all | solution.py:199
  129.0 14.3 %fusion.4 = f32[64,3584]{1,0:T(8,128)S(1)} fusion(bf16[64,4096]{1,0:T(8,128)(2,1)S(1)} %bitcast.149, bf16[1,3584,4096]{2,1,0:T(8,128)(2,1)} %param.26), kind=kOutput, calls=%fused_computation.4 | convolution fusion | flops 1879048192 | bytes 30801920 | tf_op jit(solution)/shard_map/dot_general | solution.py:209
  143.3 23.1 %fusion.12 = bf16[64,4096]{1,0:T(8,128)(2,1)S(1)} fusion(bf16[1,3584,4096]{2,1,0:T(8,128)(2,1)} %param.28, bf16[64,4096]{1,0:T(8,128)(2,1)S(1)} %bitcast.150, bf16[1,3584,4096]{2,1,0:T(8,128)(2,1)} %param.27, f32[64,3584]{1,0:T(8,128)S(1)} %fusion.4), kind=kOutput, calls=%fused_computation.8 | convolution fusion | flops 3759734784 | bytes 60686336 | tf_op jit(solution)/shard_map/dot_general | solution.py:216
  168.4 3.3 %all-to-all-start.2 = ((bf16[32,2,4096]{2,1,0:T(2,128)(2,1)}), bf16[32,2,4096]{2,1,0:T(2,128)(2,1)}, u32[]{:S(2)}, u32[]{:S(2)}) async-start(bf16[32,2,4096]{2,1,0:T(2,128)(2,1)} %copy.94), calls=%async_computation.2 | async-start | bytes 1048576 | tf_op jit(solution)/shard_map/all_to_all | solution.py:219
  172.3 15.3 %all-to-all-done.2 = bf16[32,2,4096]{2,1,0:T(2,128)(2,1)} async-done(((bf16[32,2,4096]{2,1,0:T(2,128)(2,1)}), bf16[32,2,4096]{2,1,0:T(2,128)(2,1)}, u32[]{:S(2)}, u32[]{:S(2)}) %all-to-all-start.2) | async-done | bytes 524320 | tf_op jit(solution)/shard_map/all_to_all | solution.py:219
  189.7 2.0 %fusion.15 = bf16[8,4096]{1,0:T(8,128)(2,1)} fusion(f32[8,4096]{1,0:T(8,128)S(1)} %bitcast.158, f32[8,32]{1,0:T(8,128)S(1)} %select_reduce_fusion.1, f32[32,4096]{1,0:T(8,128)} %reduce_sum.69), kind=kOutput, calls=%fused_computation.10 | convolution fusion | flops 12648448 | bytes 721920 | tf_op jit(solution)/shard_map/dot_general | solution.py:230
  (121 shorter events, 31.7 us)
Async XLA Ops:
  0.0 81.3 %copy-start = (bf16[512,2048]{1,0:T(8,128)(2,1)S(1)}, bf16[512,2048]{1,0:T(8,128)(2,1)}, u32[]{:S(2)}) copy-start(bf16[512,2048]{1,0:T(8,128)(2,1)} %param.23) | copy-start | bytes 6291460
  0.0 5.5 %collective-permute-start = (bf16[128,256]{1,0:T(8,128)(2,1)}, bf16[128,256]{1,0:T(8,128)(2,1)S(1)}, u32[]{:S(2)}, u32[]{:S(2)}) collective-permute-start(bf16[128,256]{1,0:T(8,128)(2,1)} %param.15), channel_id=1, source_target_pairs={{0,4},{1,5},{2,6},{3,7},{4,0},{5,1},{6,2},{7,3},{8,12},{9,13},{10,... | collective-permute-start | bytes 196616 | tf_op jit(solution)/shard_map/ppermute | solution.py:21
  6.4 8.3 %collective-permute-start.1 = (bf16[2,128,256]{2,1,0:T(8,128)(2,1)S(1)}, bf16[2,128,256]{2,1,0:T(8,128)(2,1)S(1)}, u32[]{:S(2)}, u32[]{:S(2)}) collective-permute-start(bf16[2,128,256]{2,1,0:T(8,128)(2,1)S(1)} %pad_maximum_fusion.3), channel_id=1, source_target_pairs={{0,8},{1,9},{2,10},{3,11},{4,12},{5,13},{6,14},{7,15},{8,0},{9,1},... | collective-permute-start | bytes 393224 | tf_op jit(solution)/shard_map/ppermute | solution.py:21
  14.7 5.0 %collective-permute-start.2 = (bf16[2,128,256]{2,1,0:T(8,128)(2,1)S(1)}, bf16[2,128,256]{2,1,0:T(8,128)(2,1)S(1)}, u32[]{:S(2)}, u32[]{:S(2)}) collective-permute-start(bf16[2,128,256]{2,1,0:T(8,128)(2,1)S(1)} %fusion.35), channel_id=1, source_target_pairs={{0,16},{16,0},{1,17},{17,1},{2,18},{18,2},{3,19},{19,3},{4,20},{20... | collective-permute-start | bytes 393224 | tf_op jit(solution)/shard_map/ppermute | solution.py:21
  19.9 6.4 %collective-permute-start.3 = (bf16[2,2,128,256]{3,2,1,0:T(8,128)(2,1)S(1)}, bf16[2,2,128,256]{3,2,1,0:T(8,128)(2,1)S(1)}, u32[]{:S(2)}, u32[]{:S(2)}) collective-permute-start(bf16[2,2,128,256]{3,2,1,0:T(8,128)(2,1)S(1)} %pad_maximum_fusion.1), channel_id=1, source_target_pairs={{0,2},{1,3},{2,0},{3,1},{4,6},{5,7},{6,4},{7,5},{8,10},{9,11},{10,... | collective-permute-start | bytes 786440 | tf_op jit(solution)/shard_map/ppermute | solution.py:21
  27.2 5.1 %collective-permute-start.4 = (bf16[2,2,2,128,256]{4,3,2,1,0:T(8,128)(2,1)}, bf16[2,2,2,128,256]{4,3,2,1,0:T(8,128)(2,1)S(1)}, u32[]{:S(2)}, u32[]{:S(2)}) collective-permute-start(bf16[2,2,2,128,256]{4,3,2,1,0:T(8,128)(2,1)} %pad_maximum_fusion), channel_id=1, source_target_pairs={{0,1},{1,0},{2,3},{3,2},{4,5},{5,4},{6,7},{7,6},{8,9},{9,8},{10,11... | collective-permute-start | bytes 1572872 | tf_op jit(solution)/shard_map/ppermute | solution.py:21
  37.8 3.2 %copy-start.3 = (f32[256,2,256]{2,0,1:T(8,128)}, f32[256,2,256]{2,0,1:T(8,128)S(1)}, u32[]{:S(2)}) copy-start(f32[256,2,256]{2,0,1:T(8,128)S(1)} %fusion.53) | copy-start | bytes 1572868
  38.6 7.2 %collective-permute-start.5 = (bf16[256,256]{1,0:T(8,128)(2,1)}, bf16[256,256]{1,0:T(8,128)(2,1)}, u32[]{:S(2)}, u32[]{:S(2)}) collective-permute-start(bf16[256,256]{1,0:T(8,128)(2,1)} %fusion.32), channel_id=1, source_target_pairs={{0,16},{16,0},{1,17},{17,1},{2,18},{18,2},{3,19},{19,3},{4,20},{20... | collective-permute-start | bytes 393224 | tf_op jit(solution)/shard_map/ppermute | solution.py:21
  41.0 15.3 %collective-permute-start.12 = (f32[128,256]{1,0:T(8,128)}, f32[128,256]{1,0:T(8,128)S(1)}, u32[]{:S(2)}, u32[]{:S(2)}) collective-permute-start(f32[128,256]{1,0:T(8,128)} %bitcast.146), channel_id=1, source_target_pairs={{0,16},{16,0},{1,17},{17,1},{2,18},{18,2},{3,19},{19,3},{4,20},{20... | collective-permute-start | bytes 393224 | tf_op jit(solution)/shard_map/ppermute | solution.py:21
  41.5 4.0 %copy-start.10 = (f32[512]{0:T(512)S(1)}, f32[512]{0:T(512)}, u32[]{:S(2)}) copy-start(f32[512]{0:T(512)} %param.19) | copy-start | bytes 6148
  41.5 4.1 %copy-start.11 = (f32[512]{0:T(512)S(1)}, f32[512]{0:T(512)}, u32[]{:S(2)}) copy-start(f32[512]{0:T(512)} %param.22) | copy-start | bytes 6148
  41.5 4.2 %copy-start.9 = (f32[4,512]{1,0:T(4,128)S(1)}, f32[4,512]{1,0:T(4,128)}, u32[]{:S(2)}) copy-start(f32[4,512]{1,0:T(4,128)} %param.18) | copy-start | bytes 24580
  45.5 1.7 copy-start.7
  45.5 1.9 copy-start.2
  47.3 2.2 %collective-permute-start.7 = (f32[256,32]{1,0:T(8,128)S(1)}, f32[256,32]{1,0:T(8,128)S(1)}, u32[]{:S(2)}, u32[]{:S(2)}) collective-permute-start(f32[256,32]{1,0:T(8,128)S(1)} %fusion.47), channel_id=1, source_target_pairs={{0,1},{1,0},{2,3},{3,2},{4,5},{5,4},{6,7},{7,6},{8,9},{9,8},{10,11... | collective-permute-start | bytes 98312 | tf_op jit(solution)/shard_map/ppermute | solution.py:21
  49.6 6.0 %collective-permute-start.8 = (f32[256,32]{1,0:T(8,128)S(1)}, f32[256,32]{1,0:T(8,128)S(1)}, u32[]{:S(2)}, u32[]{:S(2)}) collective-permute-start(f32[256,32]{1,0:T(8,128)S(1)} %add.131), channel_id=1, source_target_pairs={{0,2},{1,3},{2,0},{3,1},{4,6},{5,7},{6,4},{7,5},{8,10},{9,11},{10,... | collective-permute-start | bytes 98312 | tf_op jit(solution)/shard_map/ppermute | solution.py:21
  51.2 19.1 %collective-permute-start.6 = (bf16[256,256]{1,0:T(8,128)(2,1)S(1)}, bf16[256,256]{1,0:T(8,128)(2,1)S(1)}, u32[]{:S(2)}, u32[]{:S(2)}) collective-permute-start(bf16[256,256]{1,0:T(8,128)(2,1)S(1)} %fusion.33), channel_id=1, source_target_pairs={{0,16},{16,0},{1,17},{17,1},{2,18},{18,2},{3,19},{19,3},{4,20},{20... | collective-permute-start | bytes 393224 | tf_op jit(solution)/shard_map/ppermute | solution.py:21
  55.6 5.2 %collective-permute-start.9 = (f32[256,32]{1,0:T(8,128)S(1)}, f32[256,32]{1,0:T(8,128)S(1)}, u32[]{:S(2)}, u32[]{:S(2)}) collective-permute-start(f32[256,32]{1,0:T(8,128)S(1)} %add.132), channel_id=1, source_target_pairs={{0,4},{1,5},{2,6},{3,7},{4,0},{5,1},{6,2},{7,3},{8,12},{9,13},{10,... | collective-permute-start | bytes 98312 | tf_op jit(solution)/shard_map/ppermute | solution.py:21
  56.4 0.6 copy-start.4
  60.8 8.0 %collective-permute-start.10 = (f32[256,32]{1,0:T(8,128)S(1)}, f32[256,32]{1,0:T(8,128)S(1)}, u32[]{:S(2)}, u32[]{:S(2)}) collective-permute-start(f32[256,32]{1,0:T(8,128)S(1)} %add.133), channel_id=1, source_target_pairs={{0,8},{1,9},{2,10},{3,11},{4,12},{5,13},{6,14},{7,15},{8,0},{9,1},... | collective-permute-start | bytes 98312 | tf_op jit(solution)/shard_map/ppermute | solution.py:21
  68.8 5.0 %collective-permute-start.11 = (f32[256,32]{1,0:T(8,128)S(1)}, f32[256,32]{1,0:T(8,128)S(1)}, u32[]{:S(2)}, u32[]{:S(2)}) collective-permute-start(f32[256,32]{1,0:T(8,128)S(1)} %add.134), channel_id=1, source_target_pairs={{0,16},{16,0},{1,17},{17,1},{2,18},{18,2},{3,19},{19,3},{4,20},{20... | collective-permute-start | bytes 98312 | tf_op jit(solution)/shard_map/ppermute | solution.py:21
  75.4 5.0 %collective-permute-start.13 = (bf16[256,256]{1,0:T(8,128)(2,1)S(1)}, bf16[256,256]{1,0:T(8,128)(2,1)S(1)}, u32[]{:S(2)}, u32[]{:S(2)}) collective-permute-start(bf16[256,256]{1,0:T(8,128)(2,1)S(1)} %state_scan.1), channel_id=1, source_target_pairs={{0,16},{16,0},{1,17},{17,1},{2,18},{18,2},{3,19},{19,3},{4,20},{20... | collective-permute-start | bytes 393224 | tf_op jit(solution)/shard_map/ppermute | solution.py:21
  83.0 0.7 copy-start.8
  83.2 2.0 %collective-permute-start.14 = (bf16[8,2,8,2048]{3,2,1,0:T(8,128)(2,1)S(1)}, bf16[8,2,8,2048]{3,2,1,0:T(8,128)(2,1)S(1)}, u32[]{:S(2)}, u32[]{:S(2)}) collective-permute-start(bf16[8,2,8,2048]{3,2,1,0:T(8,128)(2,1)S(1)} %bitcast.161), channel_id=1, source_target_pairs={{0,1},{1,0},{2,3},{3,2},{4,5},{5,4},{6,7},{7,6},{8,9},{9,8},{10,11... | collective-permute-start | bytes 1572872 | tf_op jit(solution)/shard_map/ppermute | solution.py:21
  83.7 8.2 %collective-permute-start.16 = (s32[8,2]{0,1:T(2,128)S(1)}, s32[8,2]{0,1:T(2,128)S(1)}, u32[]{:S(2)}, u32[]{:S(2)}) collective-permute-start(s32[8,2]{0,1:T(2,128)S(1)} %copy-done.8), channel_id=1, source_target_pairs={{0,16},{16,0},{1,17},{17,1},{2,18},{18,2},{3,19},{19,3},{4,20},{20... | collective-permute-start | bytes 200 | tf_op jit(solution)/shard_map/ppermute | solution.py:21
  86.1 20.5 %all-to-all-start = ((bf16[8,2,8,2048]{3,2,1,0:T(8,128)(2,1)}), bf16[8,2,8,2048]{3,2,1,0:T(8,128)(2,1)S(1)}, u32[]{:S(2)}, u32[]{:S(2)}) async-start(bf16[8,2,8,2048]{3,2,1,0:T(8,128)(2,1)} %fusion.18), calls=%async_computation | async-start | bytes 1048576 | tf_op jit(solution)/shard_map/all_to_all | solution.py:175
  106.7 7.7 %copy-start.6 = (f32[4096]{0:T(1024)S(1)}, f32[4096]{0:T(1024)}, u32[]{:S(2)}) copy-start(f32[4096]{0:T(1024)} %param.24) | copy-start | bytes 49156
  108.9 19.6 %all-to-all-start.1 = ((bf16[32,4,2048]{2,1,0:T(4,128)(2,1)}), bf16[32,4,2048]{2,1,0:T(4,128)(2,1)S(1)}, u32[]{:S(2)}, u32[]{:S(2)}) async-start(bf16[32,4,2048]{2,1,0:T(4,128)(2,1)} %reshape.141), calls=%async_computation.1 | async-start | bytes 1048576 | tf_op jit(solution)/shard_map/all_to_all | solution.py:199
  112.8 5.8 %collective-permute-start.15 = (bf16[8,2048]{1,0:T(8,128)(2,1)S(1)}, bf16[8,2048]{1,0:T(8,128)(2,1)S(1)}, u32[]{:S(2)}, u32[]{:S(2)}) collective-permute-start(bf16[8,2048]{1,0:T(8,128)(2,1)S(1)} %dynamic-slice_bitcast_fusion), channel_id=1, source_target_pairs={{0,16},{16,0},{1,17},{17,1},{2,18},{18,2},{3,19},{19,3},{4,20},{20... | collective-permute-start | bytes 98312 | tf_op jit(solution)/shard_map/ppermute | solution.py:21
  166.4 5.4 %copy-start.5 = (bf16[4096,16]{0,1:T(8,128)(2,1)S(1)}, bf16[4096,16]{0,1:T(8,128)(2,1)}, u32[]{:S(2)}) copy-start(bf16[4096,16]{0,1:T(8,128)(2,1)} %param.25) | copy-start | bytes 393220
  168.4 19.2 %all-to-all-start.2 = ((bf16[32,2,4096]{2,1,0:T(2,128)(2,1)}), bf16[32,2,4096]{2,1,0:T(2,128)(2,1)}, u32[]{:S(2)}, u32[]{:S(2)}) async-start(bf16[32,2,4096]{2,1,0:T(2,128)(2,1)} %copy.94), calls=%async_computation.2 | async-start | bytes 1048576 | tf_op jit(solution)/shard_map/all_to_all | solution.py:219
  171.7 20.0 %copy-start.1 = (bf16[512,2048]{1,0:T(8,128)(2,1)S(1)}, bf16[512,2048]{1,0:T(8,128)(2,1)}, u32[]{:S(2)}) copy-start(bf16[512,2048]{1,0:T(8,128)(2,1)} %param.23) | copy-start | bytes 6291460

commit v2 on v1

v2 whole, which is shorter than its diff:
```python
import functools

import jax
import jax.numpy as jnp
from jax import lax
from jax.experimental import pallas as pl
from jax.experimental.pallas import tpu as pltpu
from jax.sharding import PartitionSpec as P

STATE = 16
CONV = 4
EPS = 1e-05
TOP = 2
CAP = 2
CHUNK = 64
QUARTERS = 8

precise = lax.Precision.HIGHEST
f32 = jnp.float32
bf16 = jnp.bfloat16


VMEM = pl.BlockSpec(memory_space=pltpu.VMEM)
SMEM = pl.BlockSpec(memory_space=pltpu.SMEM)
ANY = pl.BlockSpec(memory_space=pltpu.HBM)
MIB = 1024 * 1024


def limit(total):
    return pltpu.CompilerParams(vmem_limit_bytes=min(48, 8 * max(1, total // 256)) * MIB)


def dot(a, b, dims=((1,), (0,)), precision=None):
    return lax.dot_general(a, b, (dims, ((), ())), precision=precision, preferred_element_type=f32)


def partner(shard, axis, mask):
    devices = lax.axis_size(axis)
    return lax.ppermute(shard, axis, [(i, i ^ mask) for i in range(devices)])


def is_first(where, rank):
    return lax.slice(where, (0,), (1,)).reshape((1,) * rank) == 0


def gather_ctx(shard, where):
    if lax.axis_size("ctx") != 2:
        return lax.all_gather(shard, "ctx", axis=0)
    other = partner(shard, "ctx", 1)
    first = is_first(where, shard.ndim)
    return jnp.stack([jnp.where(first, shard, other), jnp.where(first, other, shard)], 0)


def swap_rows(pieces, where):
    if lax.axis_size("ctx") != 2:
        return lax.all_to_all(pieces, "ctx", split_axis=0, concat_axis=0, tiled=True)
    first = is_first(where, pieces.ndim - 1)
    own = jnp.where(first, pieces[0], pieces[1])
    other = partner(jnp.where(first, pieces[1], pieces[0]), "ctx", 1)
    return jnp.stack([jnp.where(first, own, other), jnp.where(first, other, own)], 0)


def token_planes(tokens):
    return [tokens] + [partner(tokens, "exp", mask) for mask in (4, 8, 12)]


def token_pieces(planes, where):
    size = lax.axis_size("exp")
    ctx, exp = [lax.slice(where, (i,), (i + 1,)).reshape(1, 1) for i in (0, 1)]
    near = ((exp >> 3) & 1) == ctx
    keep = jnp.stack([jnp.where(near, planes[i], planes[i + 2]) for i in (0, 1)], 0)
    give = jnp.stack([jnp.where(near, planes[i + 2], planes[i]) for i in (0, 1)], 0)
    both = [(i, i ^ (size | 2)) for i in range(2 * size)]
    found = {
        (0, 0): keep,
        (1, 0): partner(give, "ctx", 1),
        (0, 1): partner(keep, "exp", 2),
        (1, 1): lax.ppermute(give, ("ctx", "exp"), both),
    }
    pieces = []
    for (dx, dy), piece in found.items():
        pieces.append(((dx, dy, 0), piece))
        pieces.append(((dx, dy, 1), partner(piece, "exp", 1)))
    return pieces


def input_kernel(places, rows, where_ref, *refs):
    pieces, (x_ref, z_ref, x_keep, x_send, z_keep, z_send, own_ref, whole) = refs[:8], refs[8:16]
    weights, arrived = refs[16:]
    copies = [
        pltpu.make_async_copy(ref, weights.at[i], arrived.at[i]) for i, ref in enumerate((x_ref, z_ref))
    ]
    for copy in copies:
        copy.start()
    ctx, exp = where_ref[0], where_ref[1]
    for (dx, dy, dk), piece in zip(places, pieces):
        for j in range(2):
            block = (((exp >> 2) & 1) ^ j) * 4 + (((exp >> 1) & 1) ^ dy) * 2 + ((exp & 1) ^ dk)
            whole[block, ctx ^ dx] = piece[j]
    blocks, _, stretch, part = whole.shape
    everything = jnp.concatenate(
        [whole[b].reshape(2 * stretch, part) for b in range(blocks)], axis=1
    )
    for i, (keep_ref, send_ref) in enumerate(((x_keep, x_send), (z_keep, z_send))):
        copies[i].wait()
        result = dot(everything, weights[i])
        keep_ref[...] = result
        send_ref[...] = result.astype(bf16)
    own_rows = 2 * rows
    row = lax.broadcasted_iota(jnp.int32, (own_rows, 2 * stretch), 0)
    column = lax.broadcasted_iota(jnp.int32, (own_rows, 2 * stretch), 1)
    wanted = jnp.where(row >= rows, row - rows + stretch, row) + exp * rows
    pick = (column == wanted).astype(f32).astype(bf16)
    own_ref[...] = dot(pick, everything).astype(bf16)


def input_call(where, pieces, x_weight, z_weight, rows):
    stretch, part = pieces[0][1].shape[1:]
    shape = (2 * stretch, x_weight.shape[1])
    out_shape = [jax.ShapeDtypeStruct(shape, f32), jax.ShapeDtypeStruct(shape, bf16)] * 2
    out_shape.append(jax.ShapeDtypeStruct((2 * rows, x_weight.shape[0]), bf16))
    places = tuple(place for place, _ in pieces)
    return pl.pallas_call(
        functools.partial(input_kernel, places, rows),
        out_shape=out_shape,
        in_specs=[SMEM] + [VMEM] * 8 + [ANY] * 2,
        out_specs=[VMEM] * len(out_shape),
        scratch_shapes=[
            pltpu.VMEM((8, 2, stretch, part), bf16),
            pltpu.VMEM((2,) + x_weight.shape, bf16),
            pltpu.SemaphoreType.DMA((2,)),
        ],
        compiler_params=pltpu.CompilerParams(vmem_limit_bytes=14 * MIB),
        name="input_projections",
    )(where, *[piece for _, piece in pieces], x_weight, z_weight)


def conv_kernel(
    own_ref, got_ref, taps_ref, bias_ref, project_ref, mixer_ref, part_ref, padded, mixer_held, left
):
    total, width = own_ref.shape
    inner = (own_ref[...] + got_ref[...].astype(f32)).astype(bf16).astype(f32)
    padded[0:8, :] = jnp.zeros((8, width), f32)
    padded[8 : 8 + total, :] = inner
    filtered = jnp.broadcast_to(bias_ref[...], (total, width))
    for offset in range(CONV):
        first = 8 - (CONV - 1) + offset
        filtered = filtered + taps_ref[offset : offset + 1, :] * padded[first : first + total, :]
    mixer = (filtered * jax.nn.sigmoid(filtered)).astype(bf16)
    mixer_held[...] = mixer
    leaving = pltpu.make_async_copy(mixer_held, mixer_ref, left)
    leaving.start()
    part_ref[...] = dot(project_ref[...], mixer, ((1,), (1,)))
    leaving.wait()


def mixer_kernel(
    homes, group, where_ref, proj_ref, skip_ref, mixer_any, step_any, gate_any, got_any, weight_any,
    keep_any, send_ref, columns, mixed, mixer_ref, step_ref, gate_ref, got_ref, weight_ref, keep_ref,
    arrived,
):
    sources = (mixer_any, step_any, gate_any, got_any, weight_any)
    copies = [
        pltpu.make_async_copy(source, ref, arrived.at[i])
        for i, (source, ref) in enumerate(
            zip(sources, (mixer_ref, step_ref, gate_ref, got_ref, weight_ref))
        )
    ]
    for copy in copies:
        copy.start()
    total, width = mixer_ref.shape
    chunk = min(CHUNK, total)
    contexts = total // (homes * group)
    rows = lax.broadcasted_iota(jnp.int32, (chunk, chunk), 0)
    cols = lax.broadcasted_iota(jnp.int32, (chunk, chunk), 1)
    causal = rows >= cols
    ones = causal.astype(f32)
    columns[...] = jnp.sum(proj_ref[...], 0).T
    low = where_ref[1] & 1
    for copy in copies[:4]:
        copy.wait()

    def step(turn, state):
        start = turn * chunk
        at = pl.ds(start if isinstance(start, int) else pl.multiple_of(start, chunk), chunk)
        decay = dot(ones, step_ref[at, :], precision=precise)
        half = 0.5 * decay[chunk - 1 : chunk, :]
        mixer = mixer_ref[at, :].astype(f32)
        raised = mixer * jnp.exp(decay - half)
        gain = columns[at, :STATE]
        read = columns[at, STATE:]
        scores = jnp.where(causal, dot(read, gain, ((1,), (1,)), precise), 0.0)
        fall = jnp.exp(-half)
        state = state * fall
        reading = jnp.exp(half - decay) * (
            dot(scores, raised, precision=precise) + dot(read, state, precision=precise)
        )
        state = fall * (state + dot(gain, raised, ((0,), (0,)), precise))
        gate = (gate_ref[at, :] + got_ref[at, :].astype(f32)).astype(bf16).astype(f32)
        result = (reading + skip_ref[...] * mixer) * (gate * jax.nn.sigmoid(gate))
        for i in range(chunk // group):
            number = turn * (chunk // group) + i
            home, context = number % homes, number // homes
            place = ((home % 2) * (homes // 2) + home // 2) * contexts + context
            place = place * group
            if not isinstance(place, int):
                place = pl.multiple_of(place, group)
            mixed[pl.ds(place, group), :] = result[i * group : (i + 1) * group, :]
        return state

    state = jnp.zeros((STATE, width), f32)
    turns = total // chunk
    if turns <= 4:
        for turn in range(turns):
            state = step(turn, state)
    else:
        lax.fori_loop(0, turns, step, state)
    part = total // 2
    mine = mixed[pl.ds(pl.multiple_of(low * part, part), part), :].astype(bf16)
    other = mixed[pl.ds(pl.multiple_of((1 - low) * part, part), part), :].astype(bf16)
    copies[4].wait()
    keep_ref[...] = dot(mine, weight_ref[...]).astype(bf16)
    leaving = pltpu.make_async_copy(keep_ref, keep_any, arrived.at[5])
    leaving.start()
    send_ref[...] = dot(other, weight_ref[...]).astype(bf16)
    leaving.wait()


def pair_kernel(keep_any, got_ref, out_ref, keep_ref, arrived):
    copy = pltpu.make_async_copy(keep_any, keep_ref, arrived)
    copy.start()
    copy.wait()
    out_ref[...] = (keep_ref[...].astype(f32) + got_ref[...].astype(f32)).astype(bf16)


def dispatch_kernel(parts, pieces_ref, tokens_ref, select_ref, residual_ref, out_ref):
    projected = jnp.sum(pieces_ref[...].astype(f32), 0)
    residual = (tokens_ref[...].astype(f32) + projected).astype(bf16)
    residual_ref[...] = residual
    width = residual.shape[1] // parts
    stacked = jnp.concatenate([residual[:, q * width : (q + 1) * width] for q in range(parts)], 0)
    sent = dot(select_ref[...], stacked).astype(bf16)
    for c in range(out_ref.shape[0]):
        out_ref[c] = sent


def expert_kernel(
    contexts, parts, packed, got_ref, scale_ref, gate_any, up_any, down_any, out_ref,
    inputs, sums, held, arrived,
):
    slots, features = inputs.shape
    depth, _, block, _ = held.shape
    count = gate_any.shape[1] // block

    def copies(step):
        slot = step % depth
        return [
            pltpu.make_async_copy(
                ref.at[0, pl.ds(step * block, block)], held.at[slot, i], arrived.at[slot, i]
            )
            for i, ref in enumerate((gate_any, up_any, down_any))
        ]

    for step in range(min(depth - 1, count)):
        for copy in copies(step):
            copy.start()
    lanes = got_ref.shape[2]
    height = got_ref.shape[1]
    homes = slots // (contexts * CAP)
    row = lax.broadcasted_iota(jnp.int32, (slots, height), 0)
    column = lax.broadcasted_iota(jnp.int32, (slots, height), 1)
    cap, home = row % CAP, (row // CAP) % homes
    context = row // (CAP * homes)
    base = (home * parts * contexts + context) * CAP + cap
    for q in range(parts):
        pick = (column == base + q * contexts * CAP).astype(f32).astype(bf16)
        for c in range(contexts):
            first = (c * parts + q) * lanes
            inputs[:, first : first + lanes] = dot(pick, got_ref[c]).astype(bf16)
    wide = inputs[...].astype(f32)
    scale = lax.rsqrt(jnp.mean(wide * wide, -1, keepdims=True) + EPS)
    inputs[...] = (wide * scale * scale_ref[...]).astype(bf16)
    sums[...] = jnp.zeros_like(sums)

    for step in range(count):
        if step + depth - 1 < count:
            for copy in copies(step + depth - 1):
                copy.start()
        slot = step % depth
        gate_copy, up_copy, down_copy = copies(step)
        tokens = inputs[...]
        gate_copy.wait()
        gate = dot(tokens, held[slot, 0], ((1,), (1,)))
        up_copy.wait()
        up = dot(tokens, held[slot, 1], ((1,), (1,)))
        hidden = (gate * jax.nn.sigmoid(gate) * up).astype(bf16)
        down_copy.wait()
        sums[...] += dot(hidden, held[slot, 2])
    if not packed:
        out_ref[...] = sums[...].astype(bf16)
        return
    finished = sums[...].astype(bf16)
    width = features // QUARTERS
    stacked = jnp.concatenate(
        [finished[:, q * width : (q + 1) * width] for q in range(QUARTERS)], 0
    )
    size = slots * QUARTERS
    row = lax.broadcasted_iota(jnp.int32, (size, size), 0)
    column = lax.broadcasted_iota(jnp.int32, (size, size), 1)
    peer, q, cap = row // (QUARTERS * CAP), (row // CAP) % QUARTERS, row % CAP
    pick = (column == q * slots + peer * CAP + cap).astype(f32).astype(bf16)
    out_ref[...] = dot(pick, stacked).astype(bf16)


def home_kernel(returned_ref, combine_ref, home_ref, out_ref):
    rows = home_ref.shape[0]
    mixed = dot(combine_ref[...], returned_ref[...].astype(f32), precision=precise)
    mixed = jnp.concatenate([mixed[q * rows : (q + 1) * rows, :] for q in range(QUARTERS)], 1)
    out_ref[...] = (home_ref[...].astype(f32) + mixed).astype(bf16)


def local(
    tokens,
    input_weight,
    gate_weight,
    conv_weight,
    conv_bias,
    state_weight,
    step_size,
    skip_gain,
    output_weight,
    norm_gain,
    router_weight,
    expert_gate,
    expert_up,
    expert_down,
    expert_ids,
):
    nx, ne = lax.axis_size("ctx"), lax.axis_size("exp")
    ctx, exp = lax.axis_index("ctx"), lax.axis_index("exp")
    stretch, part = tokens.shape
    total = stretch * nx
    rows = expert_ids.shape[0]
    width = input_weight.shape[1]
    columns = output_weight.shape[1]
    experts = router_weight.shape[1]
    where = lax.optimization_barrier(jnp.stack([ctx, exp]).astype(jnp.int32))

    if nx == 2 and ne == 16:
        planes = token_planes(tokens)
        pieces = token_pieces(planes, where)
        x_own, x_send, z_own, z_send, own_tokens = input_call(
            where, pieces, input_weight, gate_weight, rows
        )
        x_send, step_size, expert_ids = lax.optimization_barrier((x_send, step_size, expert_ids))
        x_got = partner(x_send, "ctx", 1)
        z_got = partner(z_send, "ctx", 1)
    else:
        stretch_whole = lax.all_gather(tokens, "exp", axis=1, tiled=True)
        everything = lax.all_to_all(
            stretch_whole, "ctx", split_axis=1, concat_axis=0, tiled=True
        )
        own_tokens = lax.dynamic_index_in_dim(
            everything.reshape(nx, ne, rows, columns), exp, 1, keepdims=False
        ).reshape(nx * rows, columns)
        x_own = lax.psum(dot(everything, input_weight), "ctx")
        z_own = lax.psum(dot(everything, gate_weight), "ctx")
        x_got = z_got = jnp.zeros((total, width), bf16)

    everyone = gather_ctx(expert_ids, where)
    chosen = (everyone[..., None] == jnp.arange(experts, dtype=jnp.int32)).astype(jnp.int32)
    hits = chosen.reshape(nx, rows * TOP, experts)
    earlier = jnp.cumsum(hits, 1) - hits
    slot = jnp.sum(earlier * hits, -1).reshape(nx, rows, TOP)
    place = everyone * CAP + slot
    placed = place[..., None] == jnp.arange(experts * CAP, dtype=jnp.int32)
    parts = max(1, 16 // (nx * CAP))
    taken = jnp.any(placed, 2).reshape(nx, rows, experts, CAP)
    same_part = jnp.eye(parts, dtype=bool)[None, :, None, None, :, None, None]
    same_ctx = jnp.eye(nx, dtype=bool)[None, None, :, None, None, :, None]
    by_expert = taken.transpose(2, 3, 0, 1)[:, None, None, :, None, :, :]
    select = (by_expert & same_part & same_ctx).astype(bf16)
    slots = experts * nx * CAP
    select = select.reshape(slots * parts, parts * nx * rows)
    steps = gather_ctx(step_size, where).reshape(total, width)

    mixer_in, part_sum = pl.pallas_call(
        conv_kernel,
        out_shape=[
            jax.ShapeDtypeStruct((total, width), bf16),
            jax.ShapeDtypeStruct((2 * STATE, total), f32),
        ],
        in_specs=[VMEM] * 5,
        out_specs=[ANY, VMEM],
        scratch_shapes=[
            pltpu.VMEM((8 + total, width), f32),
            pltpu.VMEM((total, width), bf16),
            pltpu.SemaphoreType.DMA,
        ],
        compiler_params=limit(total),
        name="convolution",
    )(x_own, x_got, conv_weight, conv_bias[None, :], state_weight.T)

    groups = [[2 * i + k for i in range(ne // 2)] for k in range(2)]
    part_sum = part_sum + partner(part_sum, "exp", 1)
    projections = lax.all_to_all(
        jnp.broadcast_to(part_sum[None], (ne // 2,) + part_sum.shape),
        "exp", split_axis=0, concat_axis=0, tiled=True, axis_index_groups=groups,
    )
    projections, select = lax.optimization_barrier((projections, select))
    keep, send = pl.pallas_call(
        functools.partial(mixer_kernel, ne, rows),
        out_shape=[jax.ShapeDtypeStruct((total // 2, columns), bf16)] * 2,
        in_specs=[SMEM] + [VMEM] * 2 + [ANY] * 5,
        out_specs=[ANY, VMEM],
        scratch_shapes=[
            pltpu.VMEM((total, 2 * STATE), f32),
            pltpu.VMEM((total, width), f32),
            pltpu.VMEM((total, width), bf16),
            pltpu.VMEM((total, width), f32),
            pltpu.VMEM((total, width), f32),
            pltpu.VMEM((total, width), bf16),
            pltpu.VMEM(output_weight.shape, bf16),
            pltpu.VMEM((total // 2, columns), bf16),
            pltpu.SemaphoreType.DMA((6,)),
        ],
        compiler_params=limit(2 * total),
        name="state_scan_and_output",
    )(
        where, projections, skip_gain[None, :],
        mixer_in, steps, z_own, z_got, output_weight,
    )

    pair = pl.pallas_call(
        pair_kernel,
        out_shape=jax.ShapeDtypeStruct(send.shape, bf16),
        in_specs=[ANY, VMEM],
        out_specs=VMEM,
        scratch_shapes=[pltpu.VMEM(send.shape, bf16), pltpu.SemaphoreType.DMA],
        compiler_params=limit(total),
        name="pair_sum",
    )(keep, partner(send, "exp", 1))
    sums = lax.all_to_all(
        pair.reshape(ne // 2, nx * rows, columns),
        "exp", split_axis=0, concat_axis=0, tiled=True, axis_index_groups=groups,
    )

    residual, outgoing = pl.pallas_call(
        functools.partial(dispatch_kernel, parts),
        out_shape=[
            jax.ShapeDtypeStruct((nx * rows, columns), bf16),
            jax.ShapeDtypeStruct((nx, slots * parts, columns // parts), bf16),
        ],
        in_specs=[VMEM] * 3,
        out_specs=[VMEM] * 2,
        compiler_params=limit(total),
        name="residual_and_dispatch",
    )(sums, own_tokens, select)
    arrived = lax.all_to_all(
        outgoing.reshape(nx * experts, nx * CAP * parts, columns // parts),
        ("ctx", "exp"), split_axis=0, concat_axis=0, tiled=True,
    ).reshape(nx, slots * parts, columns // parts)

    hidden, features = expert_gate.shape[1:]
    block = next(b for b in (512, 448, 256, 128, 64, 32, 16) if hidden % b == 0)
    packed = nx == 2
    unit = features // QUARTERS
    peers = nx * experts
    done_shape = (peers * CAP * QUARTERS, unit) if packed else (slots, features)
    depth = 3 if packed else 2
    finished = pl.pallas_call(
        functools.partial(expert_kernel, nx, parts, packed),
        out_shape=jax.ShapeDtypeStruct(done_shape, bf16),
        in_specs=[VMEM] * 2 + [ANY] * 3,
        out_specs=VMEM,
        scratch_shapes=[
            pltpu.VMEM((slots, features), bf16),
            pltpu.VMEM((slots, features), f32),
            pltpu.VMEM((depth, 3, block, features), bf16),
            pltpu.SemaphoreType.DMA((depth, 3)),
        ],
        compiler_params=pltpu.CompilerParams(vmem_limit_bytes=52 * MIB),
        cost_estimate=pl.CostEstimate(
            flops=6 * slots * hidden * features,
            bytes_accessed=6 * hidden * features,
            transcendentals=slots * hidden,
        ),
        name="experts",
    )(arrived, norm_gain[None, :], expert_gate, expert_up, expert_down)
    if not packed:
        finished = finished.reshape(peers, CAP, QUARTERS, unit).transpose(0, 2, 1, 3)
    returned = lax.all_to_all(
        finished.reshape(peers, QUARTERS * CAP, unit),
        ("ctx", "exp"), split_axis=0, concat_axis=0, tiled=True,
    ).reshape(peers * QUARTERS * CAP, unit)

    home = swap_rows(residual.reshape(nx, rows, columns), where)
    home = home.transpose(1, 0, 2).reshape(rows, features)
    wide = home.astype(f32)
    scale = lax.rsqrt(jnp.mean(wide * wide, -1, keepdims=True) + EPS)
    normed = (wide * scale * norm_gain[None, :]).astype(bf16)
    logits = dot(normed, router_weight)
    my_choice = expert_ids[:, :, None] == jnp.arange(experts, dtype=jnp.int32)
    picked = jnp.sum(jnp.where(my_choice, logits[:, None, :], 0.0), -1)
    shares = jax.nn.sigmoid(picked - picked[:, ::-1])
    my_placed = lax.dynamic_index_in_dim(placed, ctx, 0, keepdims=False)
    combine = jnp.sum(jnp.where(my_placed, shares[:, :, None], 0.0), 1)
    combine = combine.reshape(1, rows, 1, experts, 1, CAP)
    eye = jnp.eye(QUARTERS, dtype=f32).reshape(QUARTERS, 1, 1, 1, QUARTERS, 1)
    combine = jnp.broadcast_to(combine * eye, (QUARTERS, rows, nx, experts, QUARTERS, CAP))
    combine = combine.reshape(QUARTERS * rows, peers * QUARTERS * CAP)
    return pl.pallas_call(
        home_kernel,
        out_shape=jax.ShapeDtypeStruct((rows, features), bf16),
        in_specs=[VMEM] * 3,
        out_specs=VMEM,
        compiler_params=limit(total),
        name="combine",
    )(returned, combine, home)


def solution(mesh):
    in_specs = (
        P("ctx", "exp"),
        P("ctx", "exp"),
        P("ctx", "exp"),
        P(None, "exp"),
        P("exp"),
        P("exp", None),
        P("ctx", "exp"),
        P("exp"),
        P("exp", "ctx"),
        P(),
        P(),
        P("exp", "ctx", None),
        P("exp", "ctx", None),
        P("exp", "ctx", None),
        P(("ctx", "exp"), None),
    )
    out_specs = P(("ctx", "exp"), None)
    return jax.shard_map(local, mesh=mesh, in_specs=in_specs, out_specs=out_specs, check_vma=False)
```

time: 192 us -> 153 us (0.80)
  matrix products: 46.5 us -> 0.21 us
  Pallas kernels: 1.52 us -> 40.8 us
  waiting for transfers between devices: 76.1 us -> 48.9 us
  blocking collectives: 0 us -> 18.2 us
  local copies, waits for them, and re-layouts: 22.3 us -> 9.53 us
  starting transfers between devices: 37.1 us -> 25.7 us
    dot_general x9 -> x1, matrix products: 46.5 us -> 0.21 us  [dot(): lax.dot_general(a, b, (dims, ((), ())), precision=precision, preferred_el...]
    pallas_call x1 -> x7, Pallas kernels: 1.52 us -> 40.8 us  [the longest x1 29.3 us: local(): pl.pallas_call(functools.partial(expert_kernel, nx, parts, packed), out_s...]
    ppermute x17 -> x16, waiting for transfers between devices: 38 us -> 17.6 us  [partner(): return lax.ppermute(shard, axis, [(i, i ^ mask) for i in range(devices)])]
    all_to_all x0 -> x1, blocking collectives: none -> 18.2 us  [local(): lax.all_to_all(pair.reshape(ne // 2, nx * rows, columns), 'exp', split_ax...]
    ppermute x17 -> x16, starting transfers between devices: 24.2 us -> 13.7 us  [partner(): return lax.ppermute(shard, axis, [(i, i ^ mask) for i in range(devices)])]
    all_to_all x3, waiting for transfers between devices: 38.1 us -> 29.6 us  [the longest x1 14.2 us: local(): lax.all_to_all(finished.reshape(peers, QUARTERS * CAP, unit), ('ctx', 'ex...]
    dot_general x2 -> x0, local copies, waits for them, and re-layouts: 7.98 us -> none  [the longest x1 4.01 us: local(): inner_z = jnp.dot(everything, gate_weight, preferred_element_type=f32)]
    reshape x7 -> x3, local copies, waits for them, and re-layouts: 5.88 us -> 0.69 us  [the longest x2 0.67 us: local(): combine = combine.reshape(QUARTERS * rows, peers * QUARTERS * CAP)]
  transfers between devices with their start and end apart: 20 -> 20, of which waited for: 13 -> 13; matrix products, arithmetic and copies ran while one was open for 10% -> 7% of each run, Pallas kernels for 0% -> 1%
where the time goes in v2:
time: 153 us; the launch traced here: 152 us
  waiting for transfers between devices  48.9 us (32%)
  Pallas kernels  40.8 us (27%)
  starting transfers between devices  25.7 us (17%)
  blocking collectives  18.2 us (12%)
  local copies, waits for them, and re-layouts  9.53 us (6%)
  other arithmetic  6.36 us (4%)
  between operations  2.35 us (2%)
    pallas_call x1, Pallas kernels, local(): pl.pallas_call(functools.partial(expert_kernel, nx, parts, packed), out_s...  29.3 us
    all_to_all x1, blocking collectives, local(): lax.all_to_all(pair.reshape(ne // 2, nx * rows, columns), 'exp', split_ax...  18.2 us
    ppermute x16, waiting for transfers between devices, partner(): return lax.ppermute(shard, axis, [(i, i ^ mask) for i in range(devices)])  17.6 us
    all_to_all x1, waiting for transfers between devices, local(): lax.all_to_all(finished.reshape(peers, QUARTERS * CAP, unit), ('ctx', 'ex...  14.2 us
    ppermute x16, starting transfers between devices, partner(): return lax.ppermute(shard, axis, [(i, i ^ mask) for i in range(devices)])  13.7 us
    all_to_all x1, waiting for transfers between devices, local(): lax.all_to_all(outgoing.reshape(nx * experts, nx * CAP * parts, columns /...  9.73 us
    all_to_all x1, waiting for transfers between devices, local(): lax.all_to_all(jnp.broadcast_to(part_sum[None], (ne // 2,) + part_sum.sha...  5.69 us
    unnamed x30, local copies, waits for them, and re-layouts  5.51 us
  transfers between devices with their start and end apart: 20, of which 13 were waited for; matrix products, arithmetic and copies ran while one was open for 7% of the time, Pallas kernels for 1%

profile of v2, /device:TPU:0, one launch (start us, length us, event | category | flops | bytes accessed | tf_op | source)
XLA Modules:
  0.0 152.0 jit_solution(8898618748236213828)
XLA Ops:
  0.0 3.0 %collective-permute-start.1 = (bf16[128,256]{1,0:T(8,128)(2,1)}, bf16[128,256]{1,0:T(8,128)(2,1)S(1)}, u32[]{:S(2)}, u32[]{:S(2)}) collective-permute-start(bf16[128,256]{1,0:T(8,128)(2,1)} %param.15), channel_id=1, source_target_pairs={{0,4},{1,5},{2,6},{3,7},{4,0},{5,1},{6,2},{7,3},{8,12},{9,13},{10,... | collective-permute-start | bytes 196616 | tf_op jit(solution)/shard_map/ppermute | solution.py:39
  3.0 2.6 %collective-permute-start = (bf16[128,256]{1,0:T(8,128)(2,1)}, bf16[128,256]{1,0:T(8,128)(2,1)S(1)}, u32[]{:S(2)}, u32[]{:S(2)}) collective-permute-start(bf16[128,256]{1,0:T(8,128)(2,1)} %param.15), channel_id=1, source_target_pairs={{0,8},{1,9},{2,10},{3,11},{4,12},{5,13},{6,14},{7,15},{8,0},{9,1},... | collective-permute-start | bytes 196616 | tf_op jit(solution)/shard_map/ppermute | solution.py:39
  7.7 2.8 %collective-permute-done = bf16[128,256]{1,0:T(8,128)(2,1)S(1)} collective-permute-done((bf16[128,256]{1,0:T(8,128)(2,1)}, bf16[128,256]{1,0:T(8,128)(2,1)S(1)}, u32[]{:S(2)}, u32[]{:S(2)}) %collective-permute-start) | collective-permute-done | bytes 65568 | tf_op jit(solution)/shard_map/ppermute | solution.py:39
  12.0 1.6 %collective-permute-start.6 = (bf16[2,128,256]{2,1,0:T(8,128)(2,1)S(1)}, bf16[2,128,256]{2,1,0:T(8,128)(2,1)S(1)}, u32[]{:S(2)}, u32[]{:S(2)}) collective-permute-start(bf16[2,128,256]{2,1,0:T(8,128)(2,1)S(1)} %pad_maximum_fusion.1.refs_0_), channel_id=1, source_target_pairs={{0,2},{1,3},{2,0},{3,1},{4,6},{5,7},{6,4},{7,5},{8,10},{9,11},{10,... | collective-permute-start | bytes 393224 | tf_op jit(solution)/shard_map/ppermute | solution.py:39
  13.6 1.5 collective-permute-start.8
  15.6 2.2 %collective-permute-done.6.refs_4_ = bf16[2,128,256]{2,1,0:T(8,128)(2,1)S(1)} collective-permute-done((bf16[2,128,256]{2,1,0:T(8,128)(2,1)S(1)}, bf16[2,128,256]{2,1,0:T(8,128)(2,1)S(1)}, u32[]{:S(2)}, u32[]{:S(2)}) %collective-permute-start.6) | collective-permute-done | bytes 131104 | tf_op jit(solution)/shard_map/ppermute | solution.py:39
  17.9 1.6 %collective-permute-done.8.refs_6_ = bf16[2,128,256]{2,1,0:T(8,128)(2,1)S(1)} collective-permute-done((bf16[2,128,256]{2,1,0:T(8,128)(2,1)S(1)}, bf16[2,128,256]{2,1,0:T(8,128)(2,1)S(1)}, u32[]{:S(2)}, u32[]{:S(2)}) %collective-permute-start.8) | collective-permute-done | bytes 131104 | tf_op jit(solution)/shard_map/ppermute | solution.py:78
  21.4 1.6 %copy-done.1 = bf16[2048,512]{1,0:T(8,128)(2,1)S(1)} copy-done((bf16[2048,512]{1,0:T(8,128)(2,1)S(1)}, bf16[2048,512]{1,0:T(8,128)(2,1)}, u32[]{:S(2)}) %copy-start.1) | copy-done | bytes 2097176
  23.0 1.6 %copy-done.2 = bf16[2048,512]{1,0:T(8,128)(2,1)S(1)} copy-done((bf16[2048,512]{1,0:T(8,128)(2,1)S(1)}, bf16[2048,512]{1,0:T(8,128)(2,1)}, u32[]{:S(2)}) %copy-start.2) | copy-done | bytes 2097176
  24.6 3.1 %input_projections.1 = (f32[256,512]{1,0:T(8,128)S(1)}, bf16[256,512]{1,0:T(8,128)(2,1)S(1)}, f32[256,512]{1,0:T(8,128)S(1)}, bf16[256,512]{1,0:T(8,128)(2,1)}, bf16[16,2048]{1,0:T(8,128)(2,1)S(1)}) custom-call(s32[2]{0:T(128)S(1)} %pad_add_fusion.1.where_ref, bf16[2,128,256]{2,1,0:T(8,128)(2,1)S(1)} %pad_maximum_fusion.1.refs_0_, ...), custom_call_target="tpu_custom_call" | custom-call | tf_op jit(solution)/shard_map/input_projections/pallas_call | solution.py:123
  28.3 1.4 collective-permute-start.12
  30.3 1.4 collective-permute-start.13
  33.5 5.4 %collective-permute-done.10.got_ref = bf16[256,512]{1,0:T(8,128)(2,1)S(1)} collective-permute-done((bf16[256,512]{1,0:T(8,128)(2,1)S(1)}, bf16[256,512]{1,0:T(8,128)(2,1)S(1)}, u32[]{:S(2)}, u32[]{:S(2)}) %collective-permute-start.10) | collective-permute-done | bytes 262176 | tf_op jit(solution)/shard_map/ppermute | solution.py:39
  40.5 1.1 broadcast_and_fusion
  42.5 4.9 %all-to-all-start = ((f32[8,32,256]{2,1,0:T(8,128)}), f32[8,32,256]{2,1,0:T(8,128)S(1)}, u32[]{:S(2)}, u32[]{:S(2)}) async-start(f32[8,32,256]{2,1,0:T(8,128)} %broadcast_in_dim.120), calls=%async_computation | async-start | bytes 524288 | tf_op jit(solution)/shard_map/all_to_all | solution.py:406
  47.4 1.7 %and_convert_fusion = bf16[16,4,2,2,4,2,8]{6,5,4,3,2,1,0:T(2,128)(2,1)S(1)} fusion(pred[2,2]{1,0:T(4,128)(4,1)} %iota_compare_fusion.5, pred[16,4,2,4,2,8]{5,4,3,2,1,0:T(4,128)(4,1)} %broadcast_and_fusion), kind=kLoop, calls=%fused_computation | loop fusion | flops 32768 | bytes 40964 | tf_op jit(solution)/shard_map/convert_element_type | solution.py:382
  49.0 1.0 reshape.147.select_ref
  50.0 1.1 select_bitcast_fusion.1
  51.1 5.7 %all-to-all-done.proj_ref = f32[8,32,256]{2,1,0:T(8,128)S(1)} async-done(((f32[8,32,256]{2,1,0:T(8,128)}), f32[8,32,256]{2,1,0:T(8,128)S(1)}, u32[]{:S(2)}, u32[]{:S(2)}) %all-to-all-start) | async-done | bytes 262176 | tf_op jit(solution)/shard_map/all_to_all | solution.py:406
  56.8 0.9 copy-done.6
  57.8 4.8 %state_scan_and_output.1 = (bf16[128,2048]{1,0:T(8,128)(2,1)S(1)}, bf16[128,2048]{1,0:T(8,128)(2,1)S(1)}) custom-call(s32[2]{0:T(128)S(1)} %pad_add_fusion.1.where_ref, f32[8,32,256]{2,1,0:T(8,128)S(1)} %all-to-all-done.proj_ref, f32[1,512]{1,0:T(1,128)S(1)} %bitcast.56, bf16[256,512]{1,0:T(8,128)(2,1)S(1)} %copy-done.6, f32[256,512]{1,0:T(8,128)S(1)} %bitcast.50, ...), custom_call_target="tpu_custom_call" | custom-call | tf_op jit(solution)/shard_map/state_scan_and_output/pallas_call | solution.py:411
  62.7 1.9 %collective-permute-done.15.got_ref = bf16[128,2048]{1,0:T(8,128)(2,1)S(1)} collective-permute-done((bf16[128,2048]{1,0:T(8,128)(2,1)S(1)}, bf16[128,2048]{1,0:T(8,128)(2,1)S(1)}, u32[]{:S(2)}, u32[]{:S(2)}) %collective-permute-start.15) | collective-permute-done | bytes 524320 | tf_op jit(solution)/shard_map/ppermute | solution.py:39
  64.8 18.2 %all_to_all.20.pieces_ref = bf16[8,16,2048]{2,1,0:T(8,128)(2,1)S(1)} all-to-all(bf16[8,16,2048]{2,1,0:T(8,128)(2,1)S(1)} %bitcast.48), channel_id=1, replica_groups={{0,2,4,6,8,10,12,14},{1,3,5,7,9,11,13,15},{16,18,20,22,24,26,28,30},{17..., dimensions={0} | all-to-all | bytes 1048576 | tf_op jit(solution)/shard_map/all_to_all | solution.py:443
  83.0 1.1 residual_and_dispatch.1
  84.1 3.0 %all-to-all-start.2 = ((bf16[32,16,512]{2,1,0:T(8,128)(2,1)}), bf16[32,16,512]{2,1,0:T(8,128)(2,1)S(1)}, u32[]{:S(2)}, u32[]{:S(2)}) async-start(bf16[32,16,512]{2,1,0:T(8,128)(2,1)} %bitcast.18), calls=%async_computation.2 | async-start | bytes 1048576 | tf_op jit(solution)/shard_map/all_to_all | solution.py:459
  87.1 1.8 %collective-permute-start.16 = (bf16[8,2048]{1,0:T(8,128)(2,1)S(1)}, bf16[8,2048]{1,0:T(8,128)(2,1)S(1)}, u32[]{:S(2)}, u32[]{:S(2)}) collective-permute-start(bf16[8,2048]{1,0:T(8,128)(2,1)S(1)} %broadcast_select_fusion), channel_id=1, source_target_pairs={{0,16},{16,0},{1,17},{17,1},{2,18},{18,2},{3,19},{19,3},{4,20},{20... | collective-permute-start | bytes 98312 | tf_op jit(solution)/shard_map/ppermute | solution.py:39
  88.9 4.0 %collective-permute-done.16 = bf16[8,2048]{1,0:T(8,128)(2,1)S(1)} collective-permute-done((bf16[8,2048]{1,0:T(8,128)(2,1)S(1)}, bf16[8,2048]{1,0:T(8,128)(2,1)S(1)}, u32[]{:S(2)}, u32[]{:S(2)}) %collective-permute-start.16) | collective-permute-done | bytes 32800 | tf_op jit(solution)/shard_map/ppermute | solution.py:39
  93.1 9.7 %all-to-all-done.2 = bf16[32,16,512]{2,1,0:T(8,128)(2,1)S(1)} async-done(((bf16[32,16,512]{2,1,0:T(8,128)(2,1)}), bf16[32,16,512]{2,1,0:T(8,128)(2,1)S(1)}, u32[]{:S(2)}, u32[]{:S(2)}) %all-to-all-start.2) | async-done | bytes 524320 | tf_op jit(solution)/shard_map/all_to_all | solution.py:459
  102.8 29.3 %experts.1 = bf16[512,512]{1,0:T(8,128)(2,1)} custom-call(bf16[2,256,512]{2,1,0:T(8,128)(2,1)S(1)} %bitcast.47, f32[1,4096]{1,0:T(1,128)S(1)} %bitcast.54, bf16[1,3584,4096]{2,1,0:T(8,128)(2,1)} %gate_any.1, bf16[1,3584,4096]{2,1,0:T(8,128)(2,1)} %up_any.1, bf16[1,3584,4096]{2,1,0:T(8,128)(2,1)} %down_any.1), custom_call_target="tpu_custom_call" | custom-call | flops 5637144576 | bytes 88080384 | tf_op jit(solution)/shard_map/experts/pallas_call | solution.py:471
  132.1 2.6 %all-to-all-start.3 = ((bf16[32,16,512]{2,1,0:T(8,128)(2,1)}), bf16[32,16,512]{2,1,0:T(8,128)(2,1)S(1)}, u32[]{:S(2)}, u32[]{:S(2)}) async-start(bf16[32,16,512]{2,1,0:T(8,128)(2,1)} %bitcast.21), calls=%async_computation.3 | async-start | bytes 1048576 | tf_op jit(solution)/shard_map/all_to_all | solution.py:492
  136.5 14.2 %all-to-all-done.3 = bf16[32,16,512]{2,1,0:T(8,128)(2,1)S(1)} async-done(((bf16[32,16,512]{2,1,0:T(8,128)(2,1)}), bf16[32,16,512]{2,1,0:T(8,128)(2,1)S(1)}, u32[]{:S(2)}, u32[]{:S(2)}) %all-to-all-start.3) | async-done | bytes 524320 | tf_op jit(solution)/shard_map/all_to_all | solution.py:492
  150.7 1.4 combine.1
  (93 shorter events, 11.5 us)
Async XLA Ops:
  0.0 134.8 %copy-start = (bf16[4096,16]{0,1:T(8,128)(2,1)S(1)}, bf16[4096,16]{0,1:T(8,128)(2,1)}, u32[]{:S(2)}) copy-start(bf16[4096,16]{0,1:T(8,128)(2,1)} %param.25) | copy-start | bytes 393220
  0.0 11.4 %collective-permute-start.1 = (bf16[128,256]{1,0:T(8,128)(2,1)}, bf16[128,256]{1,0:T(8,128)(2,1)S(1)}, u32[]{:S(2)}, u32[]{:S(2)}) collective-permute-start(bf16[128,256]{1,0:T(8,128)(2,1)} %param.15), channel_id=1, source_target_pairs={{0,4},{1,5},{2,6},{3,7},{4,0},{5,1},{6,2},{7,3},{8,12},{9,13},{10,... | collective-permute-start | bytes 196616 | tf_op jit(solution)/shard_map/ppermute | solution.py:39
  3.0 7.5 %collective-permute-start = (bf16[128,256]{1,0:T(8,128)(2,1)}, bf16[128,256]{1,0:T(8,128)(2,1)S(1)}, u32[]{:S(2)}, u32[]{:S(2)}) collective-permute-start(bf16[128,256]{1,0:T(8,128)(2,1)} %param.15), channel_id=1, source_target_pairs={{0,8},{1,9},{2,10},{3,11},{4,12},{5,13},{6,14},{7,15},{8,0},{9,1},... | collective-permute-start | bytes 196616 | tf_op jit(solution)/shard_map/ppermute | solution.py:39
  5.6 6.3 %collective-permute-start.2 = (bf16[128,256]{1,0:T(8,128)(2,1)}, bf16[128,256]{1,0:T(8,128)(2,1)S(1)}, u32[]{:S(2)}, u32[]{:S(2)}) collective-permute-start(bf16[128,256]{1,0:T(8,128)(2,1)} %param.15), channel_id=1, source_target_pairs={{0,12},{1,13},{2,14},{3,15},{4,8},{5,9},{6,10},{7,11},{8,4},{9,5},... | collective-permute-start | bytes 196616 | tf_op jit(solution)/shard_map/ppermute | solution.py:39
  12.0 5.9 %collective-permute-start.6 = (bf16[2,128,256]{2,1,0:T(8,128)(2,1)S(1)}, bf16[2,128,256]{2,1,0:T(8,128)(2,1)S(1)}, u32[]{:S(2)}, u32[]{:S(2)}) collective-permute-start(bf16[2,128,256]{2,1,0:T(8,128)(2,1)S(1)} %pad_maximum_fusion.1.refs_0_), channel_id=1, source_target_pairs={{0,2},{1,3},{2,0},{3,1},{4,6},{5,7},{6,4},{7,5},{8,10},{9,11},{10,... | collective-permute-start | bytes 393224 | tf_op jit(solution)/shard_map/ppermute | solution.py:39
  13.6 5.9 %collective-permute-start.8 = (bf16[2,128,256]{2,1,0:T(8,128)(2,1)S(1)}, bf16[2,128,256]{2,1,0:T(8,128)(2,1)S(1)}, u32[]{:S(2)}, u32[]{:S(2)}) collective-permute-start(bf16[2,128,256]{2,1,0:T(8,128)(2,1)S(1)} %pad_maximum_fusion.2), channel_id=1, source_target_pairs={{0,18},{1,19},{2,16},{3,17},{4,22},{5,23},{6,20},{7,21},{8,26},{9,... | collective-permute-start | bytes 393224 | tf_op jit(solution)/shard_map/ppermute | solution.py:78
  15.1 5.0 %collective-permute-start.4 = (bf16[2,128,256]{2,1,0:T(8,128)(2,1)S(1)}, bf16[2,128,256]{2,1,0:T(8,128)(2,1)S(1)}, u32[]{:S(2)}, u32[]{:S(2)}) collective-permute-start(bf16[2,128,256]{2,1,0:T(8,128)(2,1)S(1)} %pad_maximum_fusion.2), channel_id=1, source_target_pairs={{0,16},{16,0},{1,17},{17,1},{2,18},{18,2},{3,19},{19,3},{4,20},{20... | collective-permute-start | bytes 393224 | tf_op jit(solution)/shard_map/ppermute | solution.py:39
  15.6 5.7 %collective-permute-start.3 = (bf16[2,128,256]{2,1,0:T(8,128)(2,1)S(1)}, bf16[2,128,256]{2,1,0:T(8,128)(2,1)S(1)}, u32[]{:S(2)}, u32[]{:S(2)}) collective-permute-start(bf16[2,128,256]{2,1,0:T(8,128)(2,1)S(1)} %pad_maximum_fusion.1.refs_0_), channel_id=1, source_target_pairs={{0,1},{1,0},{2,3},{3,2},{4,5},{5,4},{6,7},{7,6},{8,9},{9,8},{10,11... | collective-permute-start | bytes 393224 | tf_op jit(solution)/shard_map/ppermute | solution.py:39
  17.8 3.4 %collective-permute-start.7 = (bf16[2,128,256]{2,1,0:T(8,128)(2,1)S(1)}, bf16[2,128,256]{2,1,0:T(8,128)(2,1)S(1)}, u32[]{:S(2)}, u32[]{:S(2)}) collective-permute-start(bf16[2,128,256]{2,1,0:T(8,128)(2,1)S(1)} %collective-permute-done.6.refs_4_), channel_id=1, source_target_pairs={{0,1},{1,0},{2,3},{3,2},{4,5},{5,4},{6,7},{7,6},{8,9},{9,8},{10,11... | collective-permute-start | bytes 393224 | tf_op jit(solution)/shard_map/ppermute | solution.py:39
  19.5 1.8 %collective-permute-start.9 = (bf16[2,128,256]{2,1,0:T(8,128)(2,1)S(1)}, bf16[2,128,256]{2,1,0:T(8,128)(2,1)S(1)}, u32[]{:S(2)}, u32[]{:S(2)}) collective-permute-start(bf16[2,128,256]{2,1,0:T(8,128)(2,1)S(1)} %collective-permute-done.8.refs_6_), channel_id=1, source_target_pairs={{0,1},{1,0},{2,3},{3,2},{4,5},{5,4},{6,7},{7,6},{8,9},{9,8},{10,11... | collective-permute-start | bytes 393224 | tf_op jit(solution)/shard_map/ppermute | solution.py:39
  20.0 1.3 collective-permute-start.5
  20.6 18.3 %copy-start.12 = (f32[512]{0:T(512)S(1)}, f32[512]{0:T(512)}, u32[]{:S(2)}) copy-start(f32[512]{0:T(512)} %param.19) | copy-start | bytes 6148
  21.2 7.1 %copy-start.14 = (s32[8,2]{0,1:T(2,128)S(1)}, s32[8,2]{0,1:T(2,128)}, u32[]{:S(2)}) copy-start(s32[8,2]{0,1:T(2,128)} %param.29) | copy-start | bytes 196
  21.4 1.6 %copy-start.1 = (bf16[2048,512]{1,0:T(8,128)(2,1)S(1)}, bf16[2048,512]{1,0:T(8,128)(2,1)}, u32[]{:S(2)}) copy-start(bf16[2048,512]{1,0:T(8,128)(2,1)} %refs_8_.1) | copy-start | bytes 6291460
  23.0 1.6 %copy-start.2 = (bf16[2048,512]{1,0:T(8,128)(2,1)S(1)}, bf16[2048,512]{1,0:T(8,128)(2,1)}, u32[]{:S(2)}) copy-start(bf16[2048,512]{1,0:T(8,128)(2,1)} %refs_9_.1) | copy-start | bytes 6291460
  24.6 14.3 %copy-start.9 = (bf16[512,32]{0,1:T(8,128)(2,1)S(1)}, bf16[512,32]{0,1:T(8,128)(2,1)}, u32[]{:S(2)}) copy-start(bf16[512,32]{0,1:T(8,128)(2,1)} %param.20) | copy-start | bytes 98308
  24.6 14.3 %copy-start.11 = (f32[4,512]{1,0:T(4,128)S(1)}, f32[4,512]{1,0:T(4,128)}, u32[]{:S(2)}) copy-start(f32[4,512]{1,0:T(4,128)} %taps_ref.1) | copy-start | bytes 24580
  28.3 4.1 %collective-permute-start.12 = (s32[8,2]{0,1:T(2,128)S(1)}, s32[8,2]{0,1:T(2,128)S(1)}, u32[]{:S(2)}, u32[]{:S(2)}) collective-permute-start(s32[8,2]{0,1:T(2,128)S(1)} %copy-done.14), channel_id=1, source_target_pairs={{0,16},{16,0},{1,17},{17,1},{2,18},{18,2},{3,19},{19,3},{4,20},{20... | collective-permute-start | bytes 200 | tf_op jit(solution)/shard_map/ppermute | solution.py:39
  29.7 9.2 %collective-permute-start.10 = (bf16[256,512]{1,0:T(8,128)(2,1)S(1)}, bf16[256,512]{1,0:T(8,128)(2,1)S(1)}, u32[]{:S(2)}, u32[]{:S(2)}) collective-permute-start(bf16[256,512]{1,0:T(8,128)(2,1)S(1)} %get-tuple-element.23), channel_id=1, source_target_pairs={{0,16},{16,0},{1,17},{17,1},{2,18},{18,2},{3,19},{19,3},{4,20},{20... | collective-permute-start | bytes 786440 | tf_op jit(solution)/shard_map/ppermute | solution.py:39
  30.3 19.7 %collective-permute-start.13 = (f32[128,512]{1,0:T(8,128)}, f32[128,512]{1,0:T(8,128)}, u32[]{:S(2)}, u32[]{:S(2)}) collective-permute-start(f32[128,512]{1,0:T(8,128)} %param.21), channel_id=1, source_target_pairs={{0,16},{16,0},{1,17},{17,1},{2,18},{18,2},{3,19},{19,3},{4,20},{20... | collective-permute-start | bytes 786440 | tf_op jit(solution)/shard_map/ppermute | solution.py:39
  31.7 25.1 %collective-permute-start.14 = (bf16[256,512]{1,0:T(8,128)(2,1)}, bf16[256,512]{1,0:T(8,128)(2,1)}, u32[]{:S(2)}, u32[]{:S(2)}) collective-permute-start(bf16[256,512]{1,0:T(8,128)(2,1)} %get-tuple-element.30), channel_id=1, source_target_pairs={{0,16},{16,0},{1,17},{17,1},{2,18},{18,2},{3,19},{19,3},{4,20},{20... | collective-permute-start | bytes 786440 | tf_op jit(solution)/shard_map/ppermute | solution.py:39
  40.5 1.2 collective-permute-start.11
  41.7 15.1 %copy-start.3 = (bf16[512,2048]{1,0:T(8,128)(2,1)S(1)}, bf16[512,2048]{1,0:T(8,128)(2,1)}, u32[]{:S(2)}) copy-start(bf16[512,2048]{1,0:T(8,128)(2,1)} %weight_any.1) | copy-start | bytes 6291460
  41.7 15.1 %copy-start.13 = (f32[512]{0:T(512)S(1)}, f32[512]{0:T(512)}, u32[]{:S(2)}) copy-start(f32[512]{0:T(512)} %param.22) | copy-start | bytes 6148
  42.5 14.3 %all-to-all-start = ((f32[8,32,256]{2,1,0:T(8,128)}), f32[8,32,256]{2,1,0:T(8,128)S(1)}, u32[]{:S(2)}, u32[]{:S(2)}) async-start(f32[8,32,256]{2,1,0:T(8,128)} %broadcast_in_dim.120), calls=%async_computation | async-start | bytes 524288 | tf_op jit(solution)/shard_map/all_to_all | solution.py:406
  62.6 20.4 %copy-start.4 = (bf16[256,64]{1,0:T(8,128)(2,1)S(1)}, bf16[256,64]{1,0:T(8,128)(2,1)}, u32[]{:S(2)}) copy-start(bf16[256,64]{1,0:T(8,128)(2,1)} %reshape.147.select_ref) | copy-start | bytes 98308
  62.6 20.4 %copy-start.8 = (bf16[16,2048]{1,0:T(8,128)(2,1)S(1)}, bf16[16,2048]{1,0:T(8,128)(2,1)}, u32[]{:S(2)}) copy-start(bf16[16,2048]{1,0:T(8,128)(2,1)} %copy-done.7) | copy-start | bytes 196612
  62.6 2.0 %collective-permute-start.15 = (bf16[128,2048]{1,0:T(8,128)(2,1)S(1)}, bf16[128,2048]{1,0:T(8,128)(2,1)S(1)}, u32[]{:S(2)}, u32[]{:S(2)}) collective-permute-start(bf16[128,2048]{1,0:T(8,128)(2,1)S(1)} %get-tuple-element.32), channel_id=1, source_target_pairs={{0,1},{1,0},{2,3},{3,2},{4,5},{5,4},{6,7},{7,6},{8,9},{9,8},{10,11... | collective-permute-start | bytes 1572872 | tf_op jit(solution)/shard_map/ppermute | solution.py:39
  64.6 38.2 %copy-start.10 = (f32[4096]{0:T(1024)S(1)}, f32[4096]{0:T(1024)}, u32[]{:S(2)}) copy-start(f32[4096]{0:T(1024)} %param.24) | copy-start | bytes 49156
  84.1 18.7 %all-to-all-start.2 = ((bf16[32,16,512]{2,1,0:T(8,128)(2,1)}), bf16[32,16,512]{2,1,0:T(8,128)(2,1)S(1)}, u32[]{:S(2)}, u32[]{:S(2)}) async-start(bf16[32,16,512]{2,1,0:T(8,128)(2,1)} %bitcast.18), calls=%async_computation.2 | async-start | bytes 1048576 | tf_op jit(solution)/shard_map/all_to_all | solution.py:459
  87.1 5.8 %collective-permute-start.16 = (bf16[8,2048]{1,0:T(8,128)(2,1)S(1)}, bf16[8,2048]{1,0:T(8,128)(2,1)S(1)}, u32[]{:S(2)}, u32[]{:S(2)}) collective-permute-start(bf16[8,2048]{1,0:T(8,128)(2,1)S(1)} %broadcast_select_fusion), channel_id=1, source_target_pairs={{0,16},{16,0},{1,17},{17,1},{2,18},{18,2},{3,19},{19,3},{4,20},{20... | collective-permute-start | bytes 98312 | tf_op jit(solution)/shard_map/ppermute | solution.py:39
  132.1 18.5 %all-to-all-start.3 = ((bf16[32,16,512]{2,1,0:T(8,128)(2,1)}), bf16[32,16,512]{2,1,0:T(8,128)(2,1)S(1)}, u32[]{:S(2)}, u32[]{:S(2)}) async-start(bf16[32,16,512]{2,1,0:T(8,128)(2,1)} %bitcast.21), calls=%async_computation.3 | async-start | bytes 1048576 | tf_op jit(solution)/shard_map/all_to_all | solution.py:492
  (3 other events, 2.3 us)

commit v3 on v2

--- a/solution.py
+++ b/solution.py
@@ -2,6 +2,7 @@
 
 import jax
 import jax.numpy as jnp
+import numpy as np
 from jax import lax
 from jax.experimental import pallas as pl
 from jax.experimental.pallas import tpu as pltpu
@@ -85,13 +86,10 @@
 
 
 def input_kernel(places, rows, where_ref, *refs):
-    pieces, (x_ref, z_ref, x_keep, x_send, z_keep, z_send, own_ref, whole) = refs[:8], refs[8:16]
-    weights, arrived = refs[16:]
-    copies = [
-        pltpu.make_async_copy(ref, weights.at[i], arrived.at[i]) for i, ref in enumerate((x_ref, z_ref))
-    ]
-    for copy in copies:
-        copy.start()
+    pieces, (weight_any, keep_ref, send_ref), rest = refs[:8], refs[8:11], refs[11:]
+    *own_refs, whole, weight_ref, arrived = rest
+    copy = pltpu.make_async_copy(weight_any, weight_ref, arrived)
+    copy.start()
     ctx, exp = where_ref[0], where_ref[1]
     for (dx, dy, dk), piece in zip(places, pieces):
         for j in range(2):
@@ -101,38 +99,39 @@
     everything = jnp.concatenate(
         [whole[b].reshape(2 * stretch, part) for b in range(blocks)], axis=1
     )
-    for i, (keep_ref, send_ref) in enumerate(((x_keep, x_send), (z_keep, z_send))):
-        copies[i].wait()
-        result = dot(everything, weights[i])
-        keep_ref[...] = result
-        send_ref[...] = result.astype(bf16)
-    own_rows = 2 * rows
-    row = lax.broadcasted_iota(jnp.int32, (own_rows, 2 * stretch), 0)
-    column = lax.broadcasted_iota(jnp.int32, (own_rows, 2 * stretch), 1)
-    wanted = jnp.where(row >= rows, row - rows + stretch, row) + exp * rows
-    pick = (column == wanted).astype(f32).astype(bf16)
-    own_ref[...] = dot(pick, everything).astype(bf16)
-
-
-def input_call(where, pieces, x_weight, z_weight, rows):
+    copy.wait()
+    result = dot(everything, weight_ref[...])
+    keep_ref[...] = result
+    send_ref[...] = result.astype(bf16)
+    for own_ref in own_refs:
+        own_rows = 2 * rows
+        row = lax.broadcasted_iota(jnp.int32, (own_rows, 2 * stretch), 0)
+        column = lax.broadcasted_iota(jnp.int32, (own_rows, 2 * stretch), 1)
+        wanted = jnp.where(row >= rows, row - rows + stretch, row) + exp * rows
+        pick = (column == wanted).astype(f32).astype(bf16)
+        own_ref[...] = dot(pick, everything).astype(bf16)
+
+
+def input_call(where, pieces, weight, rows, with_own, name):
     stretch, part = pieces[0][1].shape[1:]
-    shape = (2 * stretch, x_weight.shape[1])
-    out_shape = [jax.ShapeDtypeStruct(shape, f32), jax.ShapeDtypeStruct(shape, bf16)] * 2
-    out_shape.append(jax.ShapeDtypeStruct((2 * rows, x_weight.shape[0]), bf16))
+    shape = (2 * stretch, weight.shape[1])
+    out_shape = [jax.ShapeDtypeStruct(shape, f32), jax.ShapeDtypeStruct(shape, bf16)]
+    if with_own:
+        out_shape.append(jax.ShapeDtypeStruct((2 * rows, weight.shape[0]), bf16))
     places = tuple(place for place, _ in pieces)
     return pl.pallas_call(
         functools.partial(input_kernel, places, rows),
         out_shape=out_shape,
-        in_specs=[SMEM] + [VMEM] * 8 + [ANY] * 2,
+        in_specs=[SMEM] + [VMEM] * 8 + [ANY],
         out_specs=[VMEM] * len(out_shape),
         scratch_shapes=[
             pltpu.VMEM((8, 2, stretch, part), bf16),
-            pltpu.VMEM((2,) + x_weight.shape, bf16),
-            pltpu.SemaphoreType.DMA((2,)),
+            pltpu.VMEM(weight.shape, bf16),
+            pltpu.SemaphoreType.DMA,
         ],
-        compiler_params=pltpu.CompilerParams(vmem_limit_bytes=14 * MIB),
-        name="input_projections",
-    )(where, *[piece for _, piece in pieces], x_weight, z_weight)
+        compiler_params=pltpu.CompilerParams(vmem_limit_bytes=12 * MIB),
+        name=name,
+    )(where, *[piece for _, piece in pieces], weight)
 
 
 def conv_kernel(
@@ -155,16 +154,23 @@
 
 
 def mixer_kernel(
-    homes, group, where_ref, proj_ref, skip_ref, mixer_any, step_any, gate_any, got_any, weight_any,
-    keep_any, send_ref, columns, mixed, mixer_ref, step_ref, gate_ref, got_ref, weight_ref, keep_ref,
-    arrived,
+    homes, group, where_ref, proj_ref, skip_ref, mixer_any, gate_any, got_any, weight_any, *refs
 ):
-    sources = (mixer_any, step_any, gate_any, got_any, weight_any)
+    (
+        *step_anys, keep_any, send_ref, columns, mixed, mixer_ref, gate_ref, got_ref, weight_ref,
+        step_ref, keep_ref, arrived,
+    ) = refs
+    pairs = [(mixer_any, mixer_ref), (gate_any, gate_ref), (got_any, got_ref)]
+    if len(step_anys) == 1:
+        pairs.append((step_anys[0], step_ref))
+    else:
+        stretch = step_anys[0].shape[0]
+        for i, step_any in enumerate(step_anys):
+            first = pl.multiple_of((where_ref[0] ^ i) * stretch, stretch)
+            pairs.append((step_any, step_ref.at[pl.ds(first, stretch)]))
+    pairs.append((weight_any, weight_ref))
     copies = [
-        pltpu.make_async_copy(source, ref, arrived.at[i])
-        for i, (source, ref) in enumerate(
-            zip(sources, (mixer_ref, step_ref, gate_ref, got_ref, weight_ref))
-        )
+        pltpu.make_async_copy(source, ref, arrived.at[i]) for i, (source, ref) in enumerate(pairs)
     ]
     for copy in copies:
         copy.start()
@@ -177,7 +183,7 @@
     ones = causal.astype(f32)
     columns[...] = jnp.sum(proj_ref[...], 0).T
     low = where_ref[1] & 1
-    for copy in copies[:4]:
+    for copy in copies[:-1]:
         copy.wait()
 
     def step(turn, state):
@@ -218,9 +224,9 @@
     part = total // 2
     mine = mixed[pl.ds(pl.multiple_of(low * part, part), part), :].astype(bf16)
     other = mixed[pl.ds(pl.multiple_of((1 - low) * part, part), part), :].astype(bf16)
-    copies[4].wait()
+    copies[-1].wait()
     keep_ref[...] = dot(mine, weight_ref[...]).astype(bf16)
-    leaving = pltpu.make_async_copy(keep_ref, keep_any, arrived.at[5])
+    leaving = pltpu.make_async_copy(keep_ref, keep_any, arrived.at[6])
     leaving.start()
     send_ref[...] = dot(other, weight_ref[...]).astype(bf16)
     leaving.wait()
@@ -349,11 +355,14 @@
     if nx == 2 and ne == 16:
         planes = token_planes(tokens)
         pieces = token_pieces(planes, where)
-        x_own, x_send, z_own, z_send, own_tokens = input_call(
-            where, pieces, input_weight, gate_weight, rows
+        x_own, x_send = input_call(where, pieces, input_weight, rows, False, "input_projection")
+        x_send, gate_weight = lax.optimization_barrier((x_send, gate_weight))
+        z_own, z_send, own_tokens = input_call(
+            where, pieces, gate_weight, rows, True, "gate_projection"
         )
-        x_send, step_size, expert_ids = lax.optimization_barrier((x_send, step_size, expert_ids))
-        x_got = partner(x_send, "ctx", 1)
+        x_got, z_send, step_size, expert_ids, where = lax.optimization_barrier(
+            (partner(x_send, "ctx", 1), z_send, step_size, expert_ids, where)
+        )
         z_got = partner(z_send, "ctx", 1)
     else:
         stretch_whole = lax.all_gather(tokens, "exp", axis=1, tiled=True)
@@ -376,13 +385,16 @@
     placed = place[..., None] == jnp.arange(experts * CAP, dtype=jnp.int32)
     parts = max(1, 16 // (nx * CAP))
     taken = jnp.any(placed, 2).reshape(nx, rows, experts, CAP)
-    same_part = jnp.eye(parts, dtype=bool)[None, :, None, None, :, None, None]
-    same_ctx = jnp.eye(nx, dtype=bool)[None, None, :, None, None, :, None]
+    same_part = np.eye(parts, dtype=bool)[None, :, None, None, :, None, None]
+    same_ctx = np.eye(nx, dtype=bool)[None, None, :, None, None, :, None]
     by_expert = taken.transpose(2, 3, 0, 1)[:, None, None, :, None, :, :]
     select = (by_expert & same_part & same_ctx).astype(bf16)
     slots = experts * nx * CAP
     select = select.reshape(slots * parts, parts * nx * rows)
-    steps = gather_ctx(step_size, where).reshape(total, width)
+    if nx == 2:
+        steps = (step_size, partner(step_size, "ctx", 1))
+    else:
+        steps = (lax.all_gather(step_size, "ctx", axis=0, tiled=True),)
 
     mixer_in, part_sum = pl.pallas_call(
         conv_kernel,
@@ -411,24 +423,24 @@
     keep, send = pl.pallas_call(
         functools.partial(mixer_kernel, ne, rows),
         out_shape=[jax.ShapeDtypeStruct((total // 2, columns), bf16)] * 2,
-        in_specs=[SMEM] + [VMEM] * 2 + [ANY] * 5,
+        in_specs=[SMEM] + [VMEM] * 2 + [ANY] * (4 + len(steps)),
         out_specs=[ANY, VMEM],
         scratch_shapes=[
             pltpu.VMEM((total, 2 * STATE), f32),
             pltpu.VMEM((total, width), f32),
             pltpu.VMEM((total, width), bf16),
             pltpu.VMEM((total, width), f32),
-            pltpu.VMEM((total, width), f32),
             pltpu.VMEM((total, width), bf16),
             pltpu.VMEM(output_weight.shape, bf16),
+            pltpu.VMEM((total, width), f32),
             pltpu.VMEM((total // 2, columns), bf16),
-            pltpu.SemaphoreType.DMA((6,)),
+            pltpu.SemaphoreType.DMA((7,)),
         ],
         compiler_params=limit(2 * total),
         name="state_scan_and_output",
     )(
         where, projections, skip_gain[None, :],
-        mixer_in, steps, z_own, z_got, output_weight,
+        mixer_in, z_own, z_got, output_weight, *steps,
     )
 
     pair = pl.pallas_call(
@@ -506,7 +518,7 @@
     my_placed = lax.dynamic_index_in_dim(placed, ctx, 0, keepdims=False)
     combine = jnp.sum(jnp.where(my_placed, shares[:, :, None], 0.0), 1)
     combine = combine.reshape(1, rows, 1, experts, 1, CAP)
-    eye = jnp.eye(QUARTERS, dtype=f32).reshape(QUARTERS, 1, 1, 1, QUARTERS, 1)
+    eye = np.eye(QUARTERS, dtype=np.float32).reshape(QUARTERS, 1, 1, 1, QUARTERS, 1)
     combine = jnp.broadcast_to(combine * eye, (QUARTERS, rows, nx, experts, QUARTERS, CAP))
     combine = combine.reshape(QUARTERS * rows, peers * QUARTERS * CAP)
     return pl.pallas_call(

time: 153 us -> 150 us (0.980)
  other arithmetic: 6.36 us -> 3.87 us
  local copies, waits for them, and re-layouts: 9.53 us -> 7.75 us
    unnamed x30 -> x32, local copies, waits for them, and re-layouts: 5.51 us -> 3.31 us
    pallas_call x1 -> x2, Pallas kernels: 3.1 us -> 3.8 us  [input_call(): pl.pallas_call(functools.partial(input_kernel, places, rows), out_shape=o...]
  transfers between devices with their start and end apart: 20 -> 20, of which waited for: 13 -> 13; matrix products, arithmetic and copies ran while one was open for 7% -> 6% of each run, Pallas kernels for 1% -> 2%
where the time goes in v3:
time: 150 us; the launch traced here: 149 us
  waiting for transfers between devices  49.5 us (33%)
  Pallas kernels  41.6 us (28%)
  starting transfers between devices  26.5 us (18%)
  blocking collectives  18.2 us (12%)
  local copies, waits for them, and re-layouts  7.75 us (5%)
  other arithmetic  3.87 us (3%)
  between operations  1.64 us (1%)
    pallas_call x1, Pallas kernels, local(): pl.pallas_call(functools.partial(expert_kernel, nx, parts, packed), out_s...  29.3 us
    ppermute x16, waiting for transfers between devices, partner(): return lax.ppermute(shard, axis, [(i, i ^ mask) for i in range(devices)])  18.2 us
    all_to_all x1, blocking collectives, local(): lax.all_to_all(pair.reshape(ne // 2, nx * rows, columns), 'exp', split_ax...  18.2 us
    ppermute x16, starting transfers between devices, partner(): return lax.ppermute(shard, axis, [(i, i ^ mask) for i in range(devices)])  14.6 us
    all_to_all x1, waiting for transfers between devices, local(): lax.all_to_all(finished.reshape(peers, QUARTERS * CAP, unit), ('ctx', 'ex...  14.2 us
    all_to_all x1, waiting for transfers between devices, local(): lax.all_to_all(outgoing.reshape(nx * experts, nx * CAP * parts, columns /...  9.73 us
    all_to_all x1, waiting for transfers between devices, local(): lax.all_to_all(jnp.broadcast_to(part_sum[None], (ne // 2,) + part_sum.sha...  5.7 us
    pallas_call x1, Pallas kernels, local(): pl.pallas_call(functools.partial(mixer_kernel, ne, rows), out_shape=[jax....  4.9 us
  transfers between devices with their start and end apart: 20, of which 13 were waited for; matrix products, arithmetic and copies ran while one was open for 6% of the time, Pallas kernels for 2%

profile of v3, /device:TPU:0, one launch (start us, length us, event | category | flops | bytes accessed | tf_op | source)
XLA Modules:
  0.0 149.2 jit_solution(14968568190126632468)
XLA Ops:
  0.0 3.0 %collective-permute-start.1 = (bf16[128,256]{1,0:T(8,128)(2,1)}, bf16[128,256]{1,0:T(8,128)(2,1)S(1)}, u32[]{:S(2)}, u32[]{:S(2)}) collective-permute-start(bf16[128,256]{1,0:T(8,128)(2,1)} %param.18), channel_id=1, source_target_pairs={{0,4},{1,5},{2,6},{3,7},{4,0},{5,1},{6,2},{7,3},{8,12},{9,13},{10,... | collective-permute-start | bytes 196616 | tf_op jit(solution)/shard_map/ppermute | solution.py:40
  3.0 2.6 %collective-permute-start = (bf16[128,256]{1,0:T(8,128)(2,1)}, bf16[128,256]{1,0:T(8,128)(2,1)S(1)}, u32[]{:S(2)}, u32[]{:S(2)}) collective-permute-start(bf16[128,256]{1,0:T(8,128)(2,1)} %param.18), channel_id=1, source_target_pairs={{0,8},{1,9},{2,10},{3,11},{4,12},{5,13},{6,14},{7,15},{8,0},{9,1},... | collective-permute-start | bytes 196616 | tf_op jit(solution)/shard_map/ppermute | solution.py:40
  7.5 3.0 %collective-permute-done = bf16[128,256]{1,0:T(8,128)(2,1)S(1)} collective-permute-done((bf16[128,256]{1,0:T(8,128)(2,1)}, bf16[128,256]{1,0:T(8,128)(2,1)S(1)}, u32[]{:S(2)}, u32[]{:S(2)}) %collective-permute-start) | collective-permute-done | bytes 65568 | tf_op jit(solution)/shard_map/ppermute | solution.py:40
  12.0 1.6 %collective-permute-start.6 = (bf16[2,128,256]{2,1,0:T(8,128)(2,1)S(1)}, bf16[2,128,256]{2,1,0:T(8,128)(2,1)S(1)}, u32[]{:S(2)}, u32[]{:S(2)}) collective-permute-start(bf16[2,128,256]{2,1,0:T(8,128)(2,1)S(1)} %pad_maximum_fusion.refs_0_), channel_id=1, source_target_pairs={{0,2},{1,3},{2,0},{3,1},{4,6},{5,7},{6,4},{7,5},{8,10},{9,11},{10,... | collective-permute-start | bytes 393224 | tf_op jit(solution)/shard_map/ppermute | solution.py:40
  13.6 1.5 %collective-permute-start.8 = (bf16[2,128,256]{2,1,0:T(8,128)(2,1)S(1)}, bf16[2,128,256]{2,1,0:T(8,128)(2,1)S(1)}, u32[]{:S(2)}, u32[]{:S(2)}) collective-permute-start(bf16[2,128,256]{2,1,0:T(8,128)(2,1)S(1)} %pad_maximum_fusion.1), channel_id=1, source_target_pairs={{0,18},{1,19},{2,16},{3,17},{4,22},{5,23},{6,20},{7,21},{8,26},{9,... | collective-permute-start | bytes 393224 | tf_op jit(solution)/shard_map/ppermute | solution.py:79
  15.6 2.2 %collective-permute-done.6.refs_4_ = bf16[2,128,256]{2,1,0:T(8,128)(2,1)S(1)} collective-permute-done((bf16[2,128,256]{2,1,0:T(8,128)(2,1)S(1)}, bf16[2,128,256]{2,1,0:T(8,128)(2,1)S(1)}, u32[]{:S(2)}, u32[]{:S(2)}) %collective-permute-start.6) | collective-permute-done | bytes 131104 | tf_op jit(solution)/shard_map/ppermute | solution.py:40
  17.9 1.6 %collective-permute-done.8.refs_6_ = bf16[2,128,256]{2,1,0:T(8,128)(2,1)S(1)} collective-permute-done((bf16[2,128,256]{2,1,0:T(8,128)(2,1)S(1)}, bf16[2,128,256]{2,1,0:T(8,128)(2,1)S(1)}, u32[]{:S(2)}, u32[]{:S(2)}) %collective-permute-start.8) | collective-permute-done | bytes 131104 | tf_op jit(solution)/shard_map/ppermute | solution.py:79
  21.4 1.6 %copy-done.1 = bf16[2048,512]{1,0:T(8,128)(2,1)S(1)} copy-done((bf16[2048,512]{1,0:T(8,128)(2,1)S(1)}, bf16[2048,512]{1,0:T(8,128)(2,1)}, u32[]{:S(2)}) %copy-start.1) | copy-done | bytes 2097176
  23.0 1.5 %input_projection.1 = (f32[256,512]{1,0:T(8,128)S(1)}, bf16[256,512]{1,0:T(8,128)(2,1)S(1)}) custom-call(s32[2]{0:T(128)S(1)} %pad_add_fusion.1.where_ref, bf16[2,128,256]{2,1,0:T(8,128)(2,1)S(1)} %pad_maximum_fusion.refs_0_, bf16[2,128,256]{2,1,0:T(8,128)(2,1)S(1)} %collective-permute-done.3.refs_1_, ...), custom_call_target="tpu_custom_call" | custom-call | tf_op jit(solution)/shard_map/input_projection/pallas_call | solution.py:122
  24.6 1.5 collective-permute-start.10
  26.1 2.3 %gate_projection.1 = (f32[256,512]{1,0:T(8,128)S(1)}, bf16[256,512]{1,0:T(8,128)(2,1)}, bf16[16,2048]{1,0:T(8,128)(2,1)S(1)}) custom-call(s32[2]{0:T(128)S(1)} %pad_add_fusion.1.where_ref, bf16[2,128,256]{2,1,0:T(8,128)(2,1)S(1)} %pad_maximum_fusion.refs_0_, bf16[2,128,256]{2,1,0:T(8,128)(2,1)S(1)} %collective-permute-done.3.refs_1_, ...), custom_call_target="tpu_custom_call" | custom-call | tf_op jit(solution)/shard_map/gate_projection/pallas_call | solution.py:122
  28.4 4.7 %collective-permute-done.10.got_ref = bf16[256,512]{1,0:T(8,128)(2,1)S(1)} collective-permute-done((bf16[256,512]{1,0:T(8,128)(2,1)S(1)}, bf16[256,512]{1,0:T(8,128)(2,1)S(1)}, u32[]{:S(2)}, u32[]{:S(2)}) %collective-permute-start.10) | collective-permute-done | bytes 262176 | tf_op jit(solution)/shard_map/ppermute | solution.py:40
  33.0 1.4 collective-permute-start.12
  34.4 0.9 convolution.3
  36.7 1.4 collective-permute-start.14
  40.0 4.9 %all-to-all-start = ((f32[8,32,256]{2,1,0:T(8,128)}), f32[8,32,256]{2,1,0:T(8,128)S(1)}, u32[]{:S(2)}, u32[]{:S(2)}) async-start(f32[8,32,256]{2,1,0:T(8,128)} %broadcast_in_dim.107), calls=%async_computation | async-start | bytes 524288 | tf_op jit(solution)/shard_map/all_to_all | solution.py:418
  45.3 1.5 %and_convert_fusion = bf16[16,4,2,2,4,2,8]{6,5,4,3,2,1,0:T(2,128)(2,1)} fusion(pred[2,2]{1,0:T(4,128)(4,1)S(1)} %copy-done.15, pred[16,4,2,4,2,8]{5,4,3,2,1,0:T(4,128)(4,1)S(1)} %broadcast_and_fusion), kind=kLoop, calls=%fused_computation | loop fusion | flops 32768 | bytes 40964 | tf_op jit(solution)/shard_map/convert_element_type | solution.py:391
  46.8 1.4 reshape.119.select_ref
  48.2 5.7 %all-to-all-done.proj_ref = f32[8,32,256]{2,1,0:T(8,128)S(1)} async-done(((f32[8,32,256]{2,1,0:T(8,128)}), f32[8,32,256]{2,1,0:T(8,128)S(1)}, u32[]{:S(2)}, u32[]{:S(2)}) %all-to-all-start) | async-done | bytes 262176 | tf_op jit(solution)/shard_map/all_to_all | solution.py:418
  54.0 0.9 copy-done.6
  54.9 4.9 %state_scan_and_output.1 = (bf16[128,2048]{1,0:T(8,128)(2,1)S(1)}, bf16[128,2048]{1,0:T(8,128)(2,1)S(1)}) custom-call(s32[2]{0:T(128)S(1)} %pad_add_fusion.1.where_ref, f32[8,32,256]{2,1,0:T(8,128)S(1)} %all-to-all-done.proj_ref, f32[1,512]{1,0:T(1,128)S(1)} %bitcast.52, bf16[256,512]{1,0:T(8,128)(2,1)S(1)} %copy-done.6, ...), custom_call_target="tpu_custom_call" | custom-call | tf_op jit(solution)/shard_map/state_scan_and_output/pallas_call | solution.py:423
  59.9 1.9 %collective-permute-done.15.got_ref = bf16[128,2048]{1,0:T(8,128)(2,1)S(1)} collective-permute-done((bf16[128,2048]{1,0:T(8,128)(2,1)S(1)}, bf16[128,2048]{1,0:T(8,128)(2,1)S(1)}, u32[]{:S(2)}, u32[]{:S(2)}) %collective-permute-start.15) | collective-permute-done | bytes 524320 | tf_op jit(solution)/shard_map/ppermute | solution.py:40
  62.0 18.2 %all_to_all.20.pieces_ref = bf16[8,16,2048]{2,1,0:T(8,128)(2,1)S(1)} all-to-all(bf16[8,16,2048]{2,1,0:T(8,128)(2,1)S(1)} %bitcast.44), channel_id=1, replica_groups={{0,2,4,6,8,10,12,14},{1,3,5,7,9,11,13,15},{16,18,20,22,24,26,28,30},{17..., dimensions={0} | all-to-all | bytes 1048576 | tf_op jit(solution)/shard_map/all_to_all | solution.py:455
  80.2 1.1 residual_and_dispatch.1
  81.3 3.0 %all-to-all-start.2 = ((bf16[32,16,512]{2,1,0:T(8,128)(2,1)}), bf16[32,16,512]{2,1,0:T(8,128)(2,1)S(1)}, u32[]{:S(2)}, u32[]{:S(2)}) async-start(bf16[32,16,512]{2,1,0:T(8,128)(2,1)} %bitcast.15), calls=%async_computation.2 | async-start | bytes 1048576 | tf_op jit(solution)/shard_map/all_to_all | solution.py:471
  84.2 1.8 %collective-permute-start.16 = (bf16[8,2048]{1,0:T(8,128)(2,1)S(1)}, bf16[8,2048]{1,0:T(8,128)(2,1)S(1)}, u32[]{:S(2)}, u32[]{:S(2)}) collective-permute-start(bf16[8,2048]{1,0:T(8,128)(2,1)S(1)} %broadcast_select_fusion), channel_id=1, source_target_pairs={{0,16},{16,0},{1,17},{17,1},{2,18},{18,2},{3,19},{19,3},{4,20},{20... | collective-permute-start | bytes 98312 | tf_op jit(solution)/shard_map/ppermute | solution.py:40
  86.1 4.0 %collective-permute-done.16 = bf16[8,2048]{1,0:T(8,128)(2,1)S(1)} collective-permute-done((bf16[8,2048]{1,0:T(8,128)(2,1)S(1)}, bf16[8,2048]{1,0:T(8,128)(2,1)S(1)}, u32[]{:S(2)}, u32[]{:S(2)}) %collective-permute-start.16) | collective-permute-done | bytes 32800 | tf_op jit(solution)/shard_map/ppermute | solution.py:40
  90.2 9.7 %all-to-all-done.2 = bf16[32,16,512]{2,1,0:T(8,128)(2,1)S(1)} async-done(((bf16[32,16,512]{2,1,0:T(8,128)(2,1)}), bf16[32,16,512]{2,1,0:T(8,128)(2,1)S(1)}, u32[]{:S(2)}, u32[]{:S(2)}) %all-to-all-start.2) | async-done | bytes 524320 | tf_op jit(solution)/shard_map/all_to_all | solution.py:471
  100.0 29.3 %experts.1 = bf16[512,512]{1,0:T(8,128)(2,1)} custom-call(bf16[2,256,512]{2,1,0:T(8,128)(2,1)S(1)} %bitcast.43, f32[1,4096]{1,0:T(1,128)S(1)} %bitcast.49, bf16[1,3584,4096]{2,1,0:T(8,128)(2,1)} %gate_any.1, bf16[1,3584,4096]{2,1,0:T(8,128)(2,1)} %up_any.1, bf16[1,3584,4096]{2,1,0:T(8,128)(2,1)} %down_any.1), custom_call_target="tpu_custom_call" | custom-call | flops 5637144576 | bytes 88080384 | tf_op jit(solution)/shard_map/experts/pallas_call | solution.py:483
  129.3 2.6 %all-to-all-start.3 = ((bf16[32,16,512]{2,1,0:T(8,128)(2,1)}), bf16[32,16,512]{2,1,0:T(8,128)(2,1)S(1)}, u32[]{:S(2)}, u32[]{:S(2)}) async-start(bf16[32,16,512]{2,1,0:T(8,128)(2,1)} %bitcast.18), calls=%async_computation.3 | async-start | bytes 1048576 | tf_op jit(solution)/shard_map/all_to_all | solution.py:504
  133.7 14.2 %all-to-all-done.3 = bf16[32,16,512]{2,1,0:T(8,128)(2,1)S(1)} async-done(((bf16[32,16,512]{2,1,0:T(8,128)(2,1)}), bf16[32,16,512]{2,1,0:T(8,128)(2,1)S(1)}, u32[]{:S(2)}, u32[]{:S(2)}) %all-to-all-start.3) | async-done | bytes 524320 | tf_op jit(solution)/shard_map/all_to_all | solution.py:504
  147.8 1.4 combine.1
  (91 shorter events, 10.2 us)
Async XLA Ops:
  0.0 131.9 %copy-start = (bf16[4096,16]{0,1:T(8,128)(2,1)S(1)}, bf16[4096,16]{0,1:T(8,128)(2,1)}, u32[]{:S(2)}) copy-start(bf16[4096,16]{0,1:T(8,128)(2,1)} %param.28) | copy-start | bytes 393220
  0.0 11.4 %collective-permute-start.1 = (bf16[128,256]{1,0:T(8,128)(2,1)}, bf16[128,256]{1,0:T(8,128)(2,1)S(1)}, u32[]{:S(2)}, u32[]{:S(2)}) collective-permute-start(bf16[128,256]{1,0:T(8,128)(2,1)} %param.18), channel_id=1, source_target_pairs={{0,4},{1,5},{2,6},{3,7},{4,0},{5,1},{6,2},{7,3},{8,12},{9,13},{10,... | collective-permute-start | bytes 196616 | tf_op jit(solution)/shard_map/ppermute | solution.py:40
  3.0 7.5 %collective-permute-start = (bf16[128,256]{1,0:T(8,128)(2,1)}, bf16[128,256]{1,0:T(8,128)(2,1)S(1)}, u32[]{:S(2)}, u32[]{:S(2)}) collective-permute-start(bf16[128,256]{1,0:T(8,128)(2,1)} %param.18), channel_id=1, source_target_pairs={{0,8},{1,9},{2,10},{3,11},{4,12},{5,13},{6,14},{7,15},{8,0},{9,1},... | collective-permute-start | bytes 196616 | tf_op jit(solution)/shard_map/ppermute | solution.py:40
  5.6 6.3 %collective-permute-start.2 = (bf16[128,256]{1,0:T(8,128)(2,1)}, bf16[128,256]{1,0:T(8,128)(2,1)S(1)}, u32[]{:S(2)}, u32[]{:S(2)}) collective-permute-start(bf16[128,256]{1,0:T(8,128)(2,1)} %param.18), channel_id=1, source_target_pairs={{0,12},{1,13},{2,14},{3,15},{4,8},{5,9},{6,10},{7,11},{8,4},{9,5},... | collective-permute-start | bytes 196616 | tf_op jit(solution)/shard_map/ppermute | solution.py:40
  12.0 5.9 %collective-permute-start.6 = (bf16[2,128,256]{2,1,0:T(8,128)(2,1)S(1)}, bf16[2,128,256]{2,1,0:T(8,128)(2,1)S(1)}, u32[]{:S(2)}, u32[]{:S(2)}) collective-permute-start(bf16[2,128,256]{2,1,0:T(8,128)(2,1)S(1)} %pad_maximum_fusion.refs_0_), channel_id=1, source_target_pairs={{0,2},{1,3},{2,0},{3,1},{4,6},{5,7},{6,4},{7,5},{8,10},{9,11},{10,... | collective-permute-start | bytes 393224 | tf_op jit(solution)/shard_map/ppermute | solution.py:40
  13.6 5.9 %collective-permute-start.8 = (bf16[2,128,256]{2,1,0:T(8,128)(2,1)S(1)}, bf16[2,128,256]{2,1,0:T(8,128)(2,1)S(1)}, u32[]{:S(2)}, u32[]{:S(2)}) collective-permute-start(bf16[2,128,256]{2,1,0:T(8,128)(2,1)S(1)} %pad_maximum_fusion.1), channel_id=1, source_target_pairs={{0,18},{1,19},{2,16},{3,17},{4,22},{5,23},{6,20},{7,21},{8,26},{9,... | collective-permute-start | bytes 393224 | tf_op jit(solution)/shard_map/ppermute | solution.py:79
  15.1 5.0 %collective-permute-start.4 = (bf16[2,128,256]{2,1,0:T(8,128)(2,1)S(1)}, bf16[2,128,256]{2,1,0:T(8,128)(2,1)S(1)}, u32[]{:S(2)}, u32[]{:S(2)}) collective-permute-start(bf16[2,128,256]{2,1,0:T(8,128)(2,1)S(1)} %pad_maximum_fusion.1), channel_id=1, source_target_pairs={{0,16},{16,0},{1,17},{17,1},{2,18},{18,2},{3,19},{19,3},{4,20},{20... | collective-permute-start | bytes 393224 | tf_op jit(solution)/shard_map/ppermute | solution.py:40
  15.6 4.4 %collective-permute-start.3 = (bf16[2,128,256]{2,1,0:T(8,128)(2,1)S(1)}, bf16[2,128,256]{2,1,0:T(8,128)(2,1)S(1)}, u32[]{:S(2)}, u32[]{:S(2)}) collective-permute-start(bf16[2,128,256]{2,1,0:T(8,128)(2,1)S(1)} %pad_maximum_fusion.refs_0_), channel_id=1, source_target_pairs={{0,1},{1,0},{2,3},{3,2},{4,5},{5,4},{6,7},{7,6},{8,9},{9,8},{10,11... | collective-permute-start | bytes 393224 | tf_op jit(solution)/shard_map/ppermute | solution.py:40
  17.8 2.2 %collective-permute-start.7 = (bf16[2,128,256]{2,1,0:T(8,128)(2,1)S(1)}, bf16[2,128,256]{2,1,0:T(8,128)(2,1)S(1)}, u32[]{:S(2)}, u32[]{:S(2)}) collective-permute-start(bf16[2,128,256]{2,1,0:T(8,128)(2,1)S(1)} %collective-permute-done.6.refs_4_), channel_id=1, source_target_pairs={{0,1},{1,0},{2,3},{3,2},{4,5},{5,4},{6,7},{7,6},{8,9},{9,8},{10,11... | collective-permute-start | bytes 393224 | tf_op jit(solution)/shard_map/ppermute | solution.py:40
  19.5 1.3 collective-permute-start.9
  20.0 1.3 collective-permute-start.5
  24.5 8.5 %copy-start.13 = (s32[8,2]{0,1:T(2,128)S(1)}, s32[8,2]{0,1:T(2,128)}, u32[]{:S(2)}) copy-start(s32[8,2]{0,1:T(2,128)} %param.32) | copy-start | bytes 196
  24.5 9.9 %copy-start.7 = (bf16[512,32]{0,1:T(8,128)(2,1)S(1)}, bf16[512,32]{0,1:T(8,128)(2,1)}, u32[]{:S(2)}) copy-start(bf16[512,32]{0,1:T(8,128)(2,1)} %param.23) | copy-start | bytes 98308
  24.5 9.9 %copy-start.9 = (f32[4,512]{1,0:T(4,128)S(1)}, f32[4,512]{1,0:T(4,128)}, u32[]{:S(2)}) copy-start(f32[4,512]{1,0:T(4,128)} %taps_ref.1) | copy-start | bytes 24580
  24.6 9.9 %copy-start.10 = (f32[512]{0:T(512)S(1)}, f32[512]{0:T(512)}, u32[]{:S(2)}) copy-start(f32[512]{0:T(512)} %param.22) | copy-start | bytes 6148
  24.6 12.1 %copy-start.4 = (f32[128,512]{1,0:T(8,128)S(1)}, f32[128,512]{1,0:T(8,128)}, u32[]{:S(2)}) copy-start(f32[128,512]{1,0:T(8,128)} %refs_0_) | copy-start | bytes 786436
  24.6 20.3 %copy-start.14 = (pred[4,4]{1,0:T(4,128)(4,1)S(1)}, pred[4,4]{1,0:T(4,128)(4,1)}, u32[]{:S(2)}) copy-start(pred[4,4]{1,0:T(4,128)(4,1)} %constant.54) | copy-start | bytes 52
  24.6 20.7 %copy-start.15 = (pred[2,2]{1,0:T(4,128)(4,1)S(1)}, pred[2,2]{1,0:T(4,128)(4,1)}, u32[]{:S(2)}) copy-start(pred[2,2]{1,0:T(4,128)(4,1)} %constant.55) | copy-start | bytes 16
  24.6 8.4 %collective-permute-start.10 = (bf16[256,512]{1,0:T(8,128)(2,1)S(1)}, bf16[256,512]{1,0:T(8,128)(2,1)S(1)}, u32[]{:S(2)}, u32[]{:S(2)}) collective-permute-start(bf16[256,512]{1,0:T(8,128)(2,1)S(1)} %get-tuple-element.26), channel_id=1, source_target_pairs={{0,16},{16,0},{1,17},{17,1},{2,18},{18,2},{3,19},{19,3},{4,20},{20... | collective-permute-start | bytes 786440 | tf_op jit(solution)/shard_map/ppermute | solution.py:40
  28.3 25.6 %copy-start.3 = (bf16[512,2048]{1,0:T(8,128)(2,1)S(1)}, bf16[512,2048]{1,0:T(8,128)(2,1)}, u32[]{:S(2)}) copy-start(bf16[512,2048]{1,0:T(8,128)(2,1)} %weight_any.1) | copy-start | bytes 6291460
  28.4 25.6 %copy-start.11 = (f32[512]{0:T(512)S(1)}, f32[512]{0:T(512)}, u32[]{:S(2)}) copy-start(f32[512]{0:T(512)} %param.25) | copy-start | bytes 6148
  33.0 5.1 %collective-permute-start.12 = (s32[8,2]{0,1:T(2,128)S(1)}, s32[8,2]{0,1:T(2,128)S(1)}, u32[]{:S(2)}, u32[]{:S(2)}) collective-permute-start(s32[8,2]{0,1:T(2,128)S(1)} %copy-done.13), channel_id=1, source_target_pairs={{0,16},{16,0},{1,17},{17,1},{2,18},{18,2},{3,19},{19,3},{4,20},{20... | collective-permute-start | bytes 200 | tf_op jit(solution)/shard_map/ppermute | solution.py:40
  36.1 3.2 %collective-permute-start.11 = (f32[32,256]{1,0:T(8,128)S(1)}, f32[32,256]{1,0:T(8,128)S(1)}, u32[]{:S(2)}, u32[]{:S(2)}) collective-permute-start(f32[32,256]{1,0:T(8,128)S(1)} %get-tuple-element.32), channel_id=1, source_target_pairs={{0,1},{1,0},{2,3},{3,2},{4,5},{5,4},{6,7},{7,6},{8,9},{9,8},{10,11... | collective-permute-start | bytes 98312 | tf_op jit(solution)/shard_map/ppermute | solution.py:40
  36.1 17.9 %collective-permute-start.13 = (bf16[256,512]{1,0:T(8,128)(2,1)}, bf16[256,512]{1,0:T(8,128)(2,1)}, u32[]{:S(2)}, u32[]{:S(2)}) collective-permute-start(bf16[256,512]{1,0:T(8,128)(2,1)} %get-tuple-element.37), channel_id=1, source_target_pairs={{0,16},{16,0},{1,17},{17,1},{2,18},{18,2},{3,19},{19,3},{4,20},{20... | collective-permute-start | bytes 786440 | tf_op jit(solution)/shard_map/ppermute | solution.py:40
  36.7 17.2 %collective-permute-start.14 = (f32[128,512]{1,0:T(8,128)S(1)}, f32[128,512]{1,0:T(8,128)}, u32[]{:S(2)}, u32[]{:S(2)}) collective-permute-start(f32[128,512]{1,0:T(8,128)S(1)} %copy-done.4), channel_id=1, source_target_pairs={{0,16},{16,0},{1,17},{17,1},{2,18},{18,2},{3,19},{19,3},{4,20},{20... | collective-permute-start | bytes 786440 | tf_op jit(solution)/shard_map/ppermute | solution.py:40
  40.0 13.9 %all-to-all-start = ((f32[8,32,256]{2,1,0:T(8,128)}), f32[8,32,256]{2,1,0:T(8,128)S(1)}, u32[]{:S(2)}, u32[]{:S(2)}) async-start(f32[8,32,256]{2,1,0:T(8,128)} %broadcast_in_dim.107), calls=%async_computation | async-start | bytes 524288 | tf_op jit(solution)/shard_map/all_to_all | solution.py:418
  59.8 2.0 %collective-permute-start.15 = (bf16[128,2048]{1,0:T(8,128)(2,1)S(1)}, bf16[128,2048]{1,0:T(8,128)(2,1)S(1)}, u32[]{:S(2)}, u32[]{:S(2)}) collective-permute-start(bf16[128,2048]{1,0:T(8,128)(2,1)S(1)} %get-tuple-element.40), channel_id=1, source_target_pairs={{0,1},{1,0},{2,3},{3,2},{4,5},{5,4},{6,7},{7,6},{8,9},{9,8},{10,11... | collective-permute-start | bytes 1572872 | tf_op jit(solution)/shard_map/ppermute | solution.py:40
  61.8 38.2 %copy-start.8 = (f32[4096]{0:T(1024)S(1)}, f32[4096]{0:T(1024)}, u32[]{:S(2)}) copy-start(f32[4096]{0:T(1024)} %param.27) | copy-start | bytes 49156
  81.3 18.7 %all-to-all-start.2 = ((bf16[32,16,512]{2,1,0:T(8,128)(2,1)}), bf16[32,16,512]{2,1,0:T(8,128)(2,1)S(1)}, u32[]{:S(2)}, u32[]{:S(2)}) async-start(bf16[32,16,512]{2,1,0:T(8,128)(2,1)} %bitcast.15), calls=%async_computation.2 | async-start | bytes 1048576 | tf_op jit(solution)/shard_map/all_to_all | solution.py:471
  84.2 5.8 %collective-permute-start.16 = (bf16[8,2048]{1,0:T(8,128)(2,1)S(1)}, bf16[8,2048]{1,0:T(8,128)(2,1)S(1)}, u32[]{:S(2)}, u32[]{:S(2)}) collective-permute-start(bf16[8,2048]{1,0:T(8,128)(2,1)S(1)} %broadcast_select_fusion), channel_id=1, source_target_pairs={{0,16},{16,0},{1,17},{17,1},{2,18},{18,2},{3,19},{19,3},{4,20},{20... | collective-permute-start | bytes 98312 | tf_op jit(solution)/shard_map/ppermute | solution.py:40
  100.0 32.6 %copy-start.12 = (f32[8,8]{0,1:T(8,128)S(1)}, f32[8,8]{0,1:T(8,128)}, u32[]{:S(2)}) copy-start(f32[8,8]{0,1:T(8,128)} %constant.56) | copy-start | bytes 772
  129.3 18.5 %all-to-all-start.3 = ((bf16[32,16,512]{2,1,0:T(8,128)(2,1)}), bf16[32,16,512]{2,1,0:T(8,128)(2,1)S(1)}, u32[]{:S(2)}, u32[]{:S(2)}) async-start(bf16[32,16,512]{2,1,0:T(8,128)(2,1)} %bitcast.18), calls=%async_computation.3 | async-start | bytes 1048576 | tf_op jit(solution)/shard_map/all_to_all | solution.py:504
  (4 other events, 6.4 us)
